TPU v7x, 512 devices: a whole 4x8x8 slice. The times are simulated.
512 devices in a mesh: gx: 128 (over y_hi, z, x), gy: 4 (over y_lo, core).
Axes of the slice: x: 4, y: 8 (y_hi: 4, y_lo: 2; y = y_hi * 2 + y_lo), z: 8, core: 2. Of those that a mesh axis runs over, the one named last changes fastest.
Arguments:
- unknown: float32 [2, 1024, 4096], P(None, 'gx', 'gy'), may hold values from -6 to 6
- height: float32 [1024, 4096], P('gx', 'gy'), may hold values from -0.4 to 0.4
- spectrum_flat: float32 [2, 4194304], P(None, ('gx', 'gy')), may hold values from -1.5 to 1.5
- spectrum_slope: float32 [2, 4194304], P(None, ('gx', 'gy')), may hold values from -15 to 15
- spectrum_curve: float32 [2, 4194304], P(None, ('gx', 'gy')), may hold values from -150 to 150
Outputs:
- applied: float32 [2, 1024, 4096], P(None, 'gx', 'gy')
All inputs are finite; a program needn't handle non-finite values.
Results may differ from a plain program's by a relative error of at most 0.0001.
Values sent between devices are 32-bit elements; how exact they have to be, the bound alone decides.
No kernel may reach another device: no remote copies, remote signals or barrier semaphores. Data moves between devices by JAX's collectives and lax.ppermute only.
A program may use at most 128 MiB of HBM per device.

v0:
```python
import functools
import math

import jax
import jax.numpy as jnp
import numpy as np
from jax import lax
from jax.experimental import pallas as pl
from jax.experimental.pallas import tpu as pltpu
from jax.sharding import PartitionSpec as P

TILE = 4
wave_number = 2.0 * math.pi
spacing = 0.1
lift_height = 0.05
area_weight = spacing * spacing
highest = lax.Precision.HIGHEST

ROWS = 8
SPAN = 1024
DEV_X = 128
DEV_Y = 4
LANES = 128
SUBS = SPAN // LANES
NARROW = 8
NX = ROWS * DEV_X
NY = SPAN * DEV_Y
HALF = ROWS * NARROW


def real_form(coeff):
    return np.block([[coeff.real, -coeff.imag], [coeff.imag, coeff.real]])


def make_tables():
    r8 = np.arange(8)
    lane = np.arange(LANES)
    eye = np.eye(8)
    row_first, row_twist, back_twist, back_last = [], [], [], []
    for q in range(DEV_Y):
        small = np.exp(-2j * np.pi * (np.outer(r8, r8) / 8 + r8[None, :] * q / 32))
        grown = np.einsum("cn,rs->rcns", small, eye).reshape(HALF, HALF)
        row_first.append(real_form(grown))
        phase = np.exp(-2j * np.pi * lane[None, :] * (r8[:, None] / 1024 + q / 4096))
        phase = np.tile(phase, (8, 1))
        row_twist.append(np.stack([phase.real, phase.imag]))
        turn = phase.conj().T
        back_twist.append(
            np.stack(
                [
                    np.concatenate([turn.real, turn.real], 1),
                    np.concatenate([-turn.imag, turn.imag], 1),
                ]
            )
        )
        wide = np.einsum("cn,rs->nrsc", small.conj(), eye).reshape(HALF, HALF)
        back_last.append(real_form(wide))
    ring = 2 * np.pi * np.outer(lane, lane) / LANES
    outer = np.concatenate([np.cos(ring), np.sin(ring)], 1)
    turn = np.exp(-2j * np.pi * np.outer(lane, np.repeat(r8, NARROW)) / NX)
    col_twist = np.stack(
        [
            np.concatenate([turn.real, turn.real], 1),
            np.concatenate([-turn.imag, turn.imag], 1),
        ]
    )
    ring8 = np.exp(-2j * np.pi * np.outer(r8, r8) / 8)
    grown = np.kron(ring8, np.eye(NARROW))
    col_small = real_form(grown).T
    col_back = real_form(grown.conj().T).T / (NX * NY)
    as32 = lambda x: np.asarray(x, np.float32)
    return {
        "row_first": as32(np.stack(row_first)),
        "row_twist": as32(np.stack(row_twist)),
        "outer": as32(outer),
        "col_twist": as32(col_twist),
        "col_small": as32(np.stack([col_small, col_back])),
        "back_twist": as32(np.stack(back_twist)),
        "back_last": as32(np.stack(back_last)),
    }


TABLES = make_tables()


def dot(left, right):
    return lax.dot_general(
        left, right, (((1,), (0,)), ((), ())), precision=highest, preferred_element_type=jnp.float32
    )


def dot_t(left, right):
    return lax.dot_general(
        left, right, (((1,), (1,)), ((), ())), precision=highest, preferred_element_type=jnp.float32
    )


def tiles_of(cells):
    return jnp.concatenate([cells[:, LANES * n : LANES * (n + 1)] for n in range(SUBS)], 0)


def swap_halves(x, sign):
    return pltpu.roll(x, 64, 1) * sign


def half_sign(first, second):
    lane = lax.broadcasted_iota(jnp.int32, (LANES, LANES), 1)
    return jnp.where(lane < 64, jnp.float32(first), jnp.float32(second))


def quarter_turn(k, direction):
    k = k % 4
    real = jnp.where(k == 0, 1.0, jnp.where(k == 2, -1.0, 0.0)).astype(jnp.float32)
    imag = jnp.where(k == 1, direction, jnp.where(k == 3, -direction, 0.0)).astype(jnp.float32)
    return real, imag


def parity_sign(q):
    return jnp.where(q % 2 == 0, 1.0, -1.0).astype(jnp.float32)


def row_spectra(q, blocks, first, twist, outer):
    sign = parity_sign(q)
    own_real, own_imag = quarter_turn(q * q, -1.0)
    mate_real, mate_imag = quarter_turn((q ^ 1) * q, -1.0)
    powers = []
    for real, imag, height in blocks:
        levels = [(real, imag)]
        for _ in range(2):
            levels.append((levels[-1][0] * height, levels[-1][1] * height))
        powers.append(levels)
    stacked = []
    for b in range(3):
        same = [powers[0][b][k] + sign * powers[1][b][k] for k in range(2)]
        mate = [powers[2][b][k] + sign * powers[3][b][k] for k in range(2)]
        merged_real = (own_real * same[0] - own_imag * same[1]) + (
            mate_real * mate[0] - mate_imag * mate[1]
        )
        merged_imag = (own_real * same[1] + own_imag * same[0]) + (
            mate_real * mate[1] + mate_imag * mate[0]
        )
        stacked.append(jnp.concatenate([merged_real, merged_imag], 0))
    stepped = dot(first, jnp.concatenate(stacked, 1))
    turned = []
    for b in range(3):
        part = stepped[:, LANES * b : LANES * (b + 1)]
        real, imag = part[:HALF], part[HALF:]
        z_real = real * twist[0] - imag * twist[1]
        z_imag = real * twist[1] + imag * twist[0]
        turned.append(
            jnp.concatenate(
                [
                    jnp.concatenate([z_real, z_imag], 1),
                    jnp.concatenate([z_imag, -z_real], 1),
                ],
                0,
            )
        )
    return dot_t(outer, jnp.concatenate(turned, 0))


def column_stage(blocks, kernels, outer, twist, small, small_back):
    plus_minus = half_sign(1.0, -1.0)
    minus_plus = half_sign(-1.0, 1.0)
    lower = [swap_halves(x, plus_minus) for x in blocks]
    stepped = dot(
        outer, jnp.concatenate([jnp.concatenate(blocks, 1), jnp.concatenate(lower, 1)], 0)
    )
    turned = []
    for b in range(3):
        part = stepped[:, LANES * b : LANES * (b + 1)]
        turned.append(part * twist[0] + pltpu.roll(part, 64, 1) * twist[1])
    spectra = dot(jnp.concatenate(turned, 0), small)
    plain = [spectra[LANES * b : LANES * (b + 1)] for b in range(3)]
    rolled = [pltpu.roll(x, 64, 1) for x in plain]

    def times(m, b):
        return kernels[m][0] * plain[b] + kernels[m][1] * rolled[b]

    mixed = [
        times(0, 0) - times(1, 1) + times(2, 2),
        times(1, 0) - 2.0 * times(2, 1),
        times(2, 0),
    ]
    back = dot(jnp.concatenate(mixed, 0), small_back)
    upper, under = [], []
    for a in range(3):
        part = back[LANES * a : LANES * (a + 1)]
        turned = part * twist[0] - pltpu.roll(part, 64, 1) * twist[1]
        upper.append(turned)
        under.append(swap_halves(turned, minus_plus))
    return dot(outer, jnp.concatenate([jnp.concatenate(upper, 1), jnp.concatenate(under, 1)], 0))


def row_inverse(q, blocks, heights, outer, twist, last):
    minus_plus = half_sign(-1.0, 1.0)
    under = [swap_halves(x, minus_plus) for x in blocks]
    stepped = dot(
        outer, jnp.concatenate([jnp.concatenate(blocks, 1), jnp.concatenate(under, 1)], 0)
    )
    turned = []
    for a in range(3):
        part = stepped[:, LANES * a : LANES * (a + 1)]
        turned.append(part * twist[0] + pltpu.roll(part, 64, 1) * twist[1])
    fields = dot_t(last, jnp.concatenate(turned, 0))
    level = [fields[:, LANES * a : LANES * (a + 1)] for a in range(3)]
    sums = []
    for m, height in zip((0, 2, 1, 3), heights):
        scale_real, scale_imag = quarter_turn((q ^ m) * q, 1.0)
        real = (level[2][:HALF] * height + level[1][:HALF]) * height + level[0][:HALF]
        imag = (level[2][HALF:] * height + level[1][HALF:]) * height + level[0][HALF:]
        sums.append((scale_real * real - scale_imag * imag, scale_real * imag + scale_imag * real))
    return sums


vmem = pl.BlockSpec(memory_space=pltpu.VMEM)


def call(body, shapes, *args, loose=0, scratch=(), flops=1_000_000, moved=1_000_000):
    specs = [vmem] * (len(args) - loose) + [pl.BlockSpec(memory_space=pl.ANY)] * loose
    return pl.pallas_call(
        body,
        out_shape=shapes,
        in_specs=specs,
        out_specs=jax.tree.map(lambda _: vmem, shapes),
        scratch_shapes=scratch,
        compiler_params=pltpu.CompilerParams(vmem_limit_bytes=40 * 1024 * 1024),
        cost_estimate=pl.CostEstimate(flops=flops, bytes_accessed=moved, transcendentals=0),
    )(*args)


def f32(*shape):
    return jax.ShapeDtypeStruct(shape, jnp.float32)


def row_kernel(own_ref, far_ref, mate_ref, diag_ref, first_ref, twist_ref, outer_ref, out_ref):
    q = lax.axis_index("gy")
    blocks = [
        [tiles_of(ref[part]) for part in range(3)] for ref in (own_ref, far_ref, mate_ref, diag_ref)
    ]
    out = row_spectra(q, blocks, first_ref[q], twist_ref[q], outer_ref[...])
    for b in range(3):
        out_ref[pl.ds(b, DEV_X, stride=3), :] = out[:, LANES * b : LANES * (b + 1)]


def table_kernel(flat_ref, slope_ref, curve_ref, out_ref):
    lane = lax.broadcasted_iota(jnp.int32, (64, LANES), 1)
    for m, ref in enumerate((flat_ref, slope_ref, curve_ref)):
        real = ref[pl.ds(0, 64, stride=2), :]
        imag = ref[pl.ds(1, 64, stride=2), :]
        for parity in range(2):
            low = lane < 64 if parity == 0 else lane >= 64
            both_real = jnp.where(low, real, pltpu.roll(real, 64, 1))
            both_imag = jnp.where(low, imag, pltpu.roll(imag, 64, 1))
            out_ref[2 * m, pl.ds(parity, 64, stride=2), :] = both_real
            out_ref[2 * m + 1, pl.ds(parity, 64, stride=2), :] = jnp.where(
                lane < 64, -both_imag, both_imag
            )


def column_kernel(in_ref, table_ref, outer_ref, twist_ref, small_ref, after_ref, out_ref):
    blocks = [in_ref[pl.ds(b, DEV_X, stride=3), :] for b in range(3)]
    kernels = [(table_ref[2 * m], table_ref[2 * m + 1]) for m in range(3)]
    out = column_stage(blocks, kernels, outer_ref[...], twist_ref, small_ref[0], small_ref[1])
    for a in range(3):
        out_ref[pl.ds(a, DEV_X, stride=3), :] = out[:, LANES * a : LANES * (a + 1)]


def inverse_kernel(
    in_ref,
    own_ref,
    far_ref,
    mate_ref,
    diag_ref,
    outer_ref,
    twist_ref,
    last_ref,
    after_ref,
    same_ref,
    mate_out_ref,
):
    q = lax.axis_index("gy")
    blocks = [in_ref[pl.ds(a, DEV_X, stride=3), :] for a in range(3)]
    heights = [tiles_of(ref[2]) for ref in (own_ref, far_ref, mate_ref, diag_ref)]
    sums = row_inverse(q, blocks, heights, outer_ref[...], twist_ref[q], last_ref[q])
    places = ((same_ref, 0), (same_ref, 1), (mate_out_ref, 0), (mate_out_ref, 1))
    for (ref, slot), pair in zip(places, sums):
        for part in range(2):
            for n in range(SUBS):
                ref[slot, part, :, LANES * n : LANES * (n + 1)] = pair[part][
                    ROWS * n : ROWS * (n + 1)
                ]


X_TOP = 1.31


def fit(function, degree):
    cheb = np.polynomial.chebyshev.Chebyshev.interpolate(function, degree, [0.0, X_TOP])
    power = cheb.convert(kind=np.polynomial.Polynomial, domain=[-1, 1], window=[-1, 1])
    moved = power(np.polynomial.Polynomial([X_TOP / 2, 1.0]))
    return [float(c) for c in moved.coef[::-1]]


COS_FIT = fit(lambda x: np.cos(wave_number * np.sqrt(x)), 10)
SIN_FIT = fit(
    lambda x: wave_number * np.sinc(2.0 * np.sqrt(x)),
    9,
)


def near_table(kinds):
    cell = np.arange(TILE)
    entries = []
    for shift_row, shift_col in kinds:
        for sr in range(TILE):
            for sc in range(TILE):
                dr = (cell + sr) % TILE - cell + TILE * shift_row
                dc = (cell + sc) % TILE - cell + TILE * shift_col
                rho2 = spacing * spacing * (dr[:, None] ** 2 + dc[None, :] ** 2)
                radius = np.sqrt(rho2 + lift_height**2)
                green = np.exp(1j * wave_number * radius) / radius
                log_slope = 1j * wave_number - 1 / radius
                first_r = green * log_slope
                second_r = green * (log_slope**2 + 1 / radius**2)
                rise = lift_height / radius
                k1 = first_r * rise
                k2 = 0.5 * (second_r * rise**2 + first_r * (1 - rise**2) / radius)
                a0 = green - lift_height * k1 + lift_height**2 * k2
                a1 = k1 - 2 * lift_height * k2
                entry = [rho2, a0.real, a1.real, k2.real, a0.imag, a1.imag, k2.imag]
                entries.append([np.tile(e, (ROWS // TILE, LANES // TILE)) for e in entry])
    return np.asarray(entries, np.float32)


SIDE_KINDS = ((0, 0), (0, -1), (0, 1))
OVER_KINDS = ((-1, 0), (1, 0))
SIDE_TABLE = near_table(SIDE_KINDS)
OVER_TABLE = near_table(OVER_KINDS)


def horner(coefficients, x):
    total = coefficients[0] * x + coefficients[1]
    for c in coefficients[2:]:
        total = total * x + c
    return total


def turned_index(axis, turn):
    place = lax.broadcasted_iota(jnp.int32, (ROWS, LANES), axis)
    within = place % TILE
    return place - within + (within + turn) % TILE


def turn_cells(x, axis, turn):
    if turn == 0:
        return x
    return jnp.take_along_axis(x, turned_index(axis, turn), axis=axis)


def meet(raised, source, table_ref, entry):
    real, imag, height = source
    w = raised - height
    v = w * w
    x = v + table_ref[entry, 0]
    u = x - X_TOP / 2
    root = lax.rsqrt(x)
    gap_real = horner(COS_FIT, u) * root - (
        table_ref[entry, 2] * w + (table_ref[entry, 3] * v + table_ref[entry, 1])
    )
    gap_imag = horner(SIN_FIT, u) - (
        table_ref[entry, 5] * w + (table_ref[entry, 6] * v + table_ref[entry, 4])
    )
    return gap_real * real - gap_imag * imag, gap_real * imag + gap_imag * real


def meet_tiles(raised, sources, table_ref):
    total_real = jnp.zeros((ROWS, LANES), jnp.float32)
    total_imag = jnp.zeros((ROWS, LANES), jnp.float32)
    for kind, source in enumerate(sources):
        for sc in range(TILE):
            column = [turn_cells(x, 1, sc) for x in source]
            for sr in range(TILE):
                cells = [turn_cells(x, 0, sr) for x in column]
                entry = (kind * TILE + sr) * TILE + sc
                real, imag = meet(raised, cells, table_ref, entry)
                total_real = total_real + real
                total_imag = total_imag + imag
    return total_real, total_imag


def side_kernel(own_ref, far_ref, mate_ref, diag_ref, table_ref, after_ref, out_ref, rows_ref, edge):
    q = lax.axis_index("gy")
    odd = q % 2 == 1
    for part in range(3):
        last = slice(SPAN - LANES, SPAN)
        first = slice(0, LANES)
        edge[0, part] = jnp.where(odd, mate_ref[part, :, last], diag_ref[part, :, last])
        edge[SUBS + 1, part] = jnp.where(odd, diag_ref[part, :, first], mate_ref[part, :, first])
        for n in range(SUBS):
            edge[n + 1, part] = own_ref[part, :, LANES * n : LANES * (n + 1)]
    rows_ref[...] = own_ref[...]
    lane = lax.broadcasted_iota(jnp.int32, (ROWS, LANES), 1)

    for n in range(SUBS):
        before = [edge[n, part] for part in range(3)]
        here = [edge[n + 1, part] for part in range(3)]
        after = [edge[n + 2, part] for part in range(3)]
        left = [
            jnp.where(lane < TILE, pltpu.roll(x, TILE, 1), pltpu.roll(y, TILE, 1))
            for x, y in zip(before, here)
        ]
        right = [
            jnp.where(
                lane < LANES - TILE,
                pltpu.roll(y, LANES - TILE, 1),
                pltpu.roll(z, LANES - TILE, 1),
            )
            for y, z in zip(here, after)
        ]
        real, imag = meet_tiles(here[2] + lift_height, (here, left, right), table_ref)
        out_ref[0, :, LANES * n : LANES * (n + 1)] = area_weight * real
        out_ref[1, :, LANES * n : LANES * (n + 1)] = area_weight * imag


def over_kernel(own_ref, up_ref, down_ref, table_ref, side_ref, after_ref, out_ref):
    sub = lax.broadcasted_iota(jnp.int32, (ROWS, LANES), 0)
    for n in range(SUBS):
        lanes = slice(LANES * n, LANES * (n + 1))
        here = [own_ref[part, :, lanes] for part in range(3)]
        swapped = [pltpu.roll(x, TILE, 0) for x in here]
        above = [
            jnp.where(sub < TILE, pltpu.roll(up_ref[part, :, lanes], TILE, 0), swapped[part])
            for part in range(3)
        ]
        below = [
            jnp.where(sub < TILE, swapped[part], pltpu.roll(down_ref[part, :, lanes], TILE, 0))
            for part in range(3)
        ]
        real, imag = meet_tiles(here[2] + lift_height, (above, below), table_ref)
        out_ref[0, :, lanes] = side_ref[0, :, lanes] + area_weight * real
        out_ref[1, :, lanes] = side_ref[1, :, lanes] + area_weight * imag


def all_to_all_x(messages):
    shaped = messages.reshape(DEV_X, 1, 3 * LANES)
    moved = lax.all_to_all(shaped, "gx", split_axis=0, concat_axis=0, tiled=True)
    return moved.reshape(3 * DEV_X, LANES)


def local(unknown, height, spectrum_flat, spectrum_slope, spectrum_curve):
    mate_pairs = [(g, g ^ 1) for g in range(DEV_Y)]
    far_pairs = [(g, g ^ 2) for g in range(DEV_Y)]
    own = jnp.concatenate([unknown, height[None]], 0)
    far = lax.ppermute(own, "gy", far_pairs)
    mate = lax.ppermute(own, "gy", mate_pairs)
    diagonal = lax.ppermute(far, "gy", mate_pairs)
    groups = (own, far, mate, diagonal)

    lined = [
        s.reshape(2, 64, LANES).transpose(1, 0, 2).reshape(2 * 64, LANES)
        for s in (spectrum_flat, spectrum_slope, spectrum_curve)
    ]
    table = call(table_kernel, f32(6, LANES, LANES), *lined)

    sent = call(
        row_kernel,
        f32(3 * DEV_X, LANES),
        *groups,
        TABLES["row_first"],
        TABLES["row_twist"],
        TABLES["outer"],
    )
    arrived = all_to_all_x(sent)
    side, rows = call(
        side_kernel,
        (f32(2, ROWS, SPAN), f32(3, ROWS, SPAN)),
        *groups,
        SIDE_TABLE,
        sent,
        loose=1,
        scratch=[pltpu.VMEM((SUBS + 2, 3, ROWS, LANES), jnp.float32)],
        flops=30_000_000,
    )
    up = lax.ppermute(rows, "gx", [(i, (i + 1) % DEV_X) for i in range(DEV_X)])
    down = lax.ppermute(rows, "gx", [((i + 1) % DEV_X, i) for i in range(DEV_X)])
    back = call(
        column_kernel,
        f32(3 * DEV_X, LANES),
        arrived,
        table,
        TABLES["outer"],
        TABLES["col_twist"],
        TABLES["col_small"],
        side,
        loose=1,
    )
    returned = all_to_all_x(back)
    near = call(
        over_kernel,
        f32(2, ROWS, SPAN),
        own,
        up,
        down,
        OVER_TABLE,
        side,
        back,
        loose=1,
        flops=20_000_000,
    )
    same, crossed = call(
        inverse_kernel,
        (f32(2, 2, ROWS, SPAN), f32(2, 2, ROWS, SPAN)),
        returned,
        *groups,
        TABLES["outer"],
        TABLES["back_twist"],
        TABLES["back_last"],
        near,
        loose=1,
    )
    from_mate = lax.ppermute(crossed, "gy", mate_pairs)
    from_far = lax.ppermute(same[1] + from_mate[1], "gy", far_pairs)
    return (same[0] + from_mate[0] + near) + from_far


def solution(mesh):
    return jax.shard_map(
        local,
        mesh=mesh,
        in_specs=(
            P(None, "gx", "gy"),
            P("gx", "gy"),
            P(None, ("gx", "gy")),
            P(None, ("gx", "gy")),
            P(None, ("gx", "gy")),
        ),
        out_specs=P(None, "gx", "gy"),
        check_vma=False,
    )
```

profile of v0, /device:TPU:1, one launch (start us, length us, event | category | flops | bytes accessed | tf_op | source)
XLA Modules:
  0.0 91.0 jit_solution(898380096825531253)
XLA Ops:
  0.0 0.0 copy-start
  0.0 1.0 %pad_maximum_fusion.own_ref = f32[3,8,1024]{2,1,0:T(8,128)S(1)} fusion(f32[1,8,1024]{2,1,0:T(8,128)} %bitcast.33, f32[2,8,1024]{2,1,0:T(8,128)} %param.14), kind=kLoop, calls=%fused_computation | loop fusion | flops 24576 | bytes 196608 | tf_op jit(solution)/shard_map/concatenate | solution.py:454
  1.0 4.0 %collective-permute-start = (f32[3,8,1024]{2,1,0:T(8,128)S(1)}, f32[3,8,1024]{2,1,0:T(8,128)S(1)}, u32[]{:S(2)}, u32[]{:S(2)}) collective-permute-start(f32[3,8,1024]{2,1,0:T(8,128)S(1)} %pad_maximum_fusion.own_ref), channel_id=1, source_target_pairs={{0,2},{1,3},{2,0},{3,1},{4,6},{5,7},{6,4},{7,5},{8,10},{9,11},{10,... | collective-permute-start | bytes 294920 | tf_op jit(solution)/shard_map/ppermute | solution.py:455
  5.0 6.7 %collective-permute-start.1 = (f32[3,8,1024]{2,1,0:T(8,128)S(1)}, f32[3,8,1024]{2,1,0:T(8,128)S(1)}, u32[]{:S(2)}, u32[]{:S(2)}) collective-permute-start(f32[3,8,1024]{2,1,0:T(8,128)S(1)} %pad_maximum_fusion.own_ref), channel_id=1, source_target_pairs={{0,1},{1,0},{2,3},{3,2},{4,5},{5,4},{6,7},{7,6},{8,9},{9,8},{10,11... | collective-permute-start | bytes 294920 | tf_op jit(solution)/shard_map/ppermute | solution.py:456
  11.7 0.0 collective-permute-done.far_ref
  11.7 4.6 %collective-permute-start.2 = (f32[3,8,1024]{2,1,0:T(8,128)S(1)}, f32[3,8,1024]{2,1,0:T(8,128)S(1)}, u32[]{:S(2)}, u32[]{:S(2)}) collective-permute-start(f32[3,8,1024]{2,1,0:T(8,128)S(1)} %collective-permute-done.far_ref), channel_id=1, source_target_pairs={{0,1},{1,0},{2,3},{3,2},{4,5},{5,4},{6,7},{7,6},{8,9},{9,8},{10,11... | collective-permute-start | bytes 294920 | tf_op jit(solution)/shard_map/ppermute | solution.py:457
  16.3 0.0 collective-permute-done.1.mate_ref
  16.3 0.9 %collective-permute-done.2.diag_ref = f32[3,8,1024]{2,1,0:T(8,128)S(1)} collective-permute-done((f32[3,8,1024]{2,1,0:T(8,128)S(1)}, f32[3,8,1024]{2,1,0:T(8,128)S(1)}, u32[]{:S(2)}, u32[]{:S(2)}) %collective-permute-start.2) | collective-permute-done | bytes 98336 | tf_op jit(solution)/shard_map/ppermute | solution.py:457
  17.2 0.0 copy-start.1
  17.2 0.9 copy-done.1
  18.1 0.0 copy-start.5
  18.1 0.9 %copy-done.5 = f32[4,128,128]{2,1,0:T(8,128)S(1)} copy-done((f32[4,128,128]{2,1,0:T(8,128)S(1)}, f32[4,128,128]{2,1,0:T(8,128)}, u32[]{:S(2)}) %copy-start.5) | copy-done | bytes 262168
  19.0 0.0 copy-start.6
  19.0 0.9 %copy-done.6 = f32[4,2,64,128]{3,2,1,0:T(8,128)S(1)} copy-done((f32[4,2,64,128]{3,2,1,0:T(8,128)S(1)}, f32[4,2,64,128]{3,2,1,0:T(8,128)}, u32[]{:S(2)}) %copy-start.6) | copy-done | bytes 262168
  20.0 1.6 %shard_map.136.after_ref = f32[384,128]{1,0:T(8,128)} custom-call(f32[3,8,1024]{2,1,0:T(8,128)S(1)} %pad_maximum_fusion.own_ref, f32[3,8,1024]{2,1,0:T(8,128)S(1)} %collective-permute-done.far_ref, f32[3,8,1024]{2,1,0:T(8,128)S(1)} %collective-permute-done.1.mate_ref, f32[3,8,1024]{2,1,0:T(8,128)S(1)} %collective-permute-done.2.diag_ref, ...), custom_call_target="tpu_custom_call" | custom-call | flops 1000000 | bytes 1000000 | tf_op jit(solution)/shard_map/pallas_call | solution.py:221
  21.6 14.6 %all-to-all-start = ((f32[128,1,384]{2,1,0:T(1,128)}), f32[128,1,384]{2,1,0:T(1,128)S(1)}, u32[]{:S(2)}, u32[]{:S(2)}) async-start(f32[128,1,384]{2,1,0:T(1,128)} %bitcast.1), calls=%async_computation | async-start | bytes 393216 | tf_op jit(solution)/shard_map/all_to_all | solution.py:447
  36.2 0.0 copy-start.2
  36.3 0.0 copy-done.10
  36.3 0.0 copy-done.11
  36.3 0.0 copy-done.12
  36.3 0.1 shard_map.137.table_ref
  36.4 0.0 copy-done
  36.4 0.0 copy-start.3
  36.4 4.2 %shard_map.138 = (f32[2,8,1024]{2,1,0:T(8,128)S(1)}, f32[3,8,1024]{2,1,0:T(8,128)S(1)}) custom-call(f32[3,8,1024]{2,1,0:T(8,128)S(1)} %pad_maximum_fusion.own_ref, f32[3,8,1024]{2,1,0:T(8,128)S(1)} %collective-permute-done.far_ref, f32[3,8,1024]{2,1,0:T(8,128)S(1)} %collective-permute-done.1.mate_ref, f32[3,8,1024]{2,1,0:T(8,128)S(1)} %collective-permute-done.2.diag_ref, ...), custom_call_target="tpu_custom_call" | custom-call | flops 30000000 | bytes 1000000 | tf_op jit(solution)/shard_map/pallas_call | solution.py:221
  40.7 0.0 copy-start.13
  40.7 0.6 copy-done.13
  41.3 9.1 %all-to-all-done = f32[128,1,384]{2,1,0:T(1,128)S(1)} async-done(((f32[128,1,384]{2,1,0:T(1,128)}), f32[128,1,384]{2,1,0:T(1,128)S(1)}, u32[]{:S(2)}, u32[]{:S(2)}) %all-to-all-start) | async-done | bytes 196640 | tf_op jit(solution)/shard_map/all_to_all | solution.py:447
  50.4 0.0 copy-done.2
  50.4 0.9 copy-done.8
  51.3 0.9 copy-done.9
  52.3 2.5 %shard_map.139.after_ref = f32[384,128]{1,0:T(8,128)} custom-call(f32[384,128]{1,0:T(8,128)S(1)} %bitcast.29, f32[6,128,128]{2,1,0:T(8,128)S(1)} %shard_map.137.table_ref, f32[128,256]{1,0:T(8,128)S(1)} %copy-done.2, f32[2,128,128]{2,1,0:T(8,128)S(1)} %copy-done.8, f32[2,128,128]{2,1,0:T(8,128)S(1)} %copy-done.9, ...), custom_call_target="tpu_custom_call" | custom-call | flops 1000000 | bytes 1000000 | tf_op jit(solution)/shard_map/pallas_call | solution.py:221
  54.8 6.7 %all-to-all-start.1 = ((f32[128,1,384]{2,1,0:T(1,128)}), f32[128,1,384]{2,1,0:T(1,128)S(1)}, u32[]{:S(2)}, u32[]{:S(2)}) async-start(f32[128,1,384]{2,1,0:T(1,128)} %bitcast.12), calls=%async_computation.1 | async-start | bytes 393216 | tf_op jit(solution)/shard_map/all_to_all | solution.py:447
  61.5 0.0 copy-done.14
  61.5 2.5 %collective-permute-start.3 = (f32[3,8,1024]{2,1,0:T(8,128)S(1)}, f32[3,8,1024]{2,1,0:T(8,128)S(1)}, u32[]{:S(2)}, u32[]{:S(2)}) collective-permute-start(f32[3,8,1024]{2,1,0:T(8,128)S(1)} %copy-done.14), channel_id=1, source_target_pairs={{0,4},{4,8},{8,12},{12,16},{16,20},{20,24},{24,28},{28,32},{32,36}... | collective-permute-start | bytes 294920 | tf_op jit(solution)/shard_map/ppermute | solution.py:485
  64.0 9.3 %collective-permute-start.4 = (f32[3,8,1024]{2,1,0:T(8,128)S(1)}, f32[3,8,1024]{2,1,0:T(8,128)S(1)}, u32[]{:S(2)}, u32[]{:S(2)}) collective-permute-start(f32[3,8,1024]{2,1,0:T(8,128)S(1)} %copy-done.14), channel_id=1, source_target_pairs={{4,0},{8,4},{12,8},{16,12},{20,16},{24,20},{28,24},{32,28},{36,32}... | collective-permute-start | bytes 294920 | tf_op jit(solution)/shard_map/ppermute | solution.py:486
  73.3 2.3 %collective-permute-done.3.up_ref = f32[3,8,1024]{2,1,0:T(8,128)S(1)} collective-permute-done((f32[3,8,1024]{2,1,0:T(8,128)S(1)}, f32[3,8,1024]{2,1,0:T(8,128)S(1)}, u32[]{:S(2)}, u32[]{:S(2)}) %collective-permute-start.3) | collective-permute-done | bytes 98336 | tf_op jit(solution)/shard_map/ppermute | solution.py:485
  75.6 0.1 collective-permute-done.4.down_ref
  75.7 0.0 copy-done.3
  75.7 2.7 %shard_map.140.after_ref = f32[2,8,1024]{2,1,0:T(8,128)S(1)} custom-call(f32[3,8,1024]{2,1,0:T(8,128)S(1)} %pad_maximum_fusion.own_ref, f32[3,8,1024]{2,1,0:T(8,128)S(1)} %collective-permute-done.3.up_ref, f32[3,8,1024]{2,1,0:T(8,128)S(1)} %collective-permute-done.4.down_ref, f32[32,7,8,128]{3,2,1,0:T(8,128)S(1)} %copy-done.3, ...), custom_call_target="tpu_custom_call" | custom-call | flops 20000000 | bytes 1000000 | tf_op jit(solution)/shard_map/pallas_call | solution.py:221
  78.4 0.0 all-to-all-done.1
  78.4 0.0 copy-done.4
  78.5 0.0 copy-done.7
  78.5 0.9 %shard_map.141 = (f32[2,2,8,1024]{3,2,1,0:T(8,128)S(1)}, f32[2,2,8,1024]{3,2,1,0:T(8,128)S(1)}) custom-call(f32[384,128]{1,0:T(8,128)S(1)} %bitcast.28, f32[3,8,1024]{2,1,0:T(8,128)S(1)} %pad_maximum_fusion.own_ref, f32[3,8,1024]{2,1,0:T(8,128)S(1)} %collective-permute-done.far_ref, f32[3,8,1024]{2,1,0:T(8,128)S(1)} %collective-permute-done.1.mate_ref, ...), custom_call_target="tpu_custom_call" | custom-call | flops 1000000 | bytes 1000000 | tf_op jit(solution)/shard_map/pallas_call | solution.py:221
  79.4 3.9 %collective-permute-start.5 = (f32[2,2,8,1024]{3,2,1,0:T(8,128)S(1)}, f32[2,2,8,1024]{3,2,1,0:T(8,128)S(1)}, u32[]{:S(2)}, u32[]{:S(2)}) collective-permute-start(f32[2,2,8,1024]{3,2,1,0:T(8,128)S(1)} %get-tuple-element.12), channel_id=1, source_target_pairs={{0,1},{1,0},{2,3},{3,2},{4,5},{5,4},{6,7},{7,6},{8,9},{9,8},{10,11... | collective-permute-start | bytes 393224 | tf_op jit(solution)/shard_map/ppermute | solution.py:522
  83.3 1.0 %collective-permute-done.5 = f32[2,2,8,1024]{3,2,1,0:T(8,128)S(1)} collective-permute-done((f32[2,2,8,1024]{3,2,1,0:T(8,128)S(1)}, f32[2,2,8,1024]{3,2,1,0:T(8,128)S(1)}, u32[]{:S(2)}, u32[]{:S(2)}) %collective-permute-start.5) | collective-permute-done | bytes 131104 | tf_op jit(solution)/shard_map/ppermute | solution.py:522
  84.3 3.9 %collective-permute-start.6 = (f32[2,8,1024]{2,1,0:T(8,128)S(1)}, f32[2,8,1024]{2,1,0:T(8,128)S(1)}, u32[]{:S(2)}, u32[]{:S(2)}) collective-permute-start(f32[2,8,1024]{2,1,0:T(8,128)S(1)} %fusion), channel_id=1, source_target_pairs={{0,2},{1,3},{2,0},{3,1},{4,6},{5,7},{6,4},{7,5},{8,10},{9,11},{10,... | collective-permute-start | bytes 196616 | tf_op jit(solution)/shard_map/ppermute | solution.py:523
  88.2 2.2 %collective-permute-done.6 = f32[2,8,1024]{2,1,0:T(8,128)S(1)} collective-permute-done((f32[2,8,1024]{2,1,0:T(8,128)S(1)}, f32[2,8,1024]{2,1,0:T(8,128)S(1)}, u32[]{:S(2)}, u32[]{:S(2)}) %collective-permute-start.6) | collective-permute-done | bytes 65568 | tf_op jit(solution)/shard_map/ppermute | solution.py:523
  90.3 0.6 fusion.3
  (9 shorter events, 0.0 us)
Async XLA Ops:
  0.0 36.4 %copy-start = (f32[48,7,8,128]{3,2,1,0:T(8,128)S(1)}, f32[48,7,8,128]{3,2,1,0:T(8,128)}, u32[]{:S(2)}) copy-start(f32[48,7,8,128]{3,2,1,0:T(8,128)} %constant.21.clone.table_ref) | copy-start | bytes 4128772
  1.0 10.7 %collective-permute-start = (f32[3,8,1024]{2,1,0:T(8,128)S(1)}, f32[3,8,1024]{2,1,0:T(8,128)S(1)}, u32[]{:S(2)}, u32[]{:S(2)}) collective-permute-start(f32[3,8,1024]{2,1,0:T(8,128)S(1)} %pad_maximum_fusion.own_ref), channel_id=1, source_target_pairs={{0,2},{1,3},{2,0},{3,1},{4,6},{5,7},{6,4},{7,5},{8,10},{9,11},{10,... | collective-permute-start | bytes 294920 | tf_op jit(solution)/shard_map/ppermute | solution.py:455
  5.0 11.3 %collective-permute-start.1 = (f32[3,8,1024]{2,1,0:T(8,128)S(1)}, f32[3,8,1024]{2,1,0:T(8,128)S(1)}, u32[]{:S(2)}, u32[]{:S(2)}) collective-permute-start(f32[3,8,1024]{2,1,0:T(8,128)S(1)} %pad_maximum_fusion.own_ref), channel_id=1, source_target_pairs={{0,1},{1,0},{2,3},{3,2},{4,5},{5,4},{6,7},{7,6},{8,9},{9,8},{10,11... | collective-permute-start | bytes 294920 | tf_op jit(solution)/shard_map/ppermute | solution.py:456
  11.7 5.5 %collective-permute-start.2 = (f32[3,8,1024]{2,1,0:T(8,128)S(1)}, f32[3,8,1024]{2,1,0:T(8,128)S(1)}, u32[]{:S(2)}, u32[]{:S(2)}) collective-permute-start(f32[3,8,1024]{2,1,0:T(8,128)S(1)} %collective-permute-done.far_ref), channel_id=1, source_target_pairs={{0,1},{1,0},{2,3},{3,2},{4,5},{5,4},{6,7},{7,6},{8,9},{9,8},{10,11... | collective-permute-start | bytes 294920 | tf_op jit(solution)/shard_map/ppermute | solution.py:457
  17.2 0.9 copy-start.1
  18.1 0.9 %copy-start.5 = (f32[4,128,128]{2,1,0:T(8,128)S(1)}, f32[4,128,128]{2,1,0:T(8,128)}, u32[]{:S(2)}) copy-start(f32[4,128,128]{2,1,0:T(8,128)} %constant.18.clone.first_ref) | copy-start | bytes 786436
  19.0 0.9 %copy-start.6 = (f32[4,2,64,128]{3,2,1,0:T(8,128)S(1)}, f32[4,2,64,128]{3,2,1,0:T(8,128)}, u32[]{:S(2)}) copy-start(f32[4,2,64,128]{3,2,1,0:T(8,128)} %constant.19.clone.twist_ref) | copy-start | bytes 786436
  20.0 16.3 %copy-start.10 = (f32[2,8192]{1,0:T(2,128)S(1)}, f32[2,8192]{1,0:T(2,128)}, u32[]{:S(2)}) copy-start(f32[2,8192]{1,0:T(2,128)} %param.16) | copy-start | bytes 196612
  20.0 16.3 %copy-start.11 = (f32[2,8192]{1,0:T(2,128)S(1)}, f32[2,8192]{1,0:T(2,128)}, u32[]{:S(2)}) copy-start(f32[2,8192]{1,0:T(2,128)} %param.17) | copy-start | bytes 196612
  20.0 16.3 %copy-start.12 = (f32[2,8192]{1,0:T(2,128)S(1)}, f32[2,8192]{1,0:T(2,128)}, u32[]{:S(2)}) copy-start(f32[2,8192]{1,0:T(2,128)} %param.18) | copy-start | bytes 196612
  21.6 28.8 %all-to-all-start = ((f32[128,1,384]{2,1,0:T(1,128)}), f32[128,1,384]{2,1,0:T(1,128)S(1)}, u32[]{:S(2)}, u32[]{:S(2)}) async-start(f32[128,1,384]{2,1,0:T(1,128)} %bitcast.1), calls=%async_computation | async-start | bytes 393216 | tf_op jit(solution)/shard_map/all_to_all | solution.py:447
  36.2 14.2 %copy-start.2 = (f32[128,256]{1,0:T(8,128)S(1)}, f32[128,256]{1,0:T(8,128)}, u32[]{:S(2)}) copy-start(f32[128,256]{1,0:T(8,128)} %constant.20.clone.outer_ref) | copy-start | bytes 393220
  36.4 39.3 %copy-start.3 = (f32[32,7,8,128]{3,2,1,0:T(8,128)S(1)}, f32[32,7,8,128]{3,2,1,0:T(8,128)}, u32[]{:S(2)}) copy-start(f32[32,7,8,128]{3,2,1,0:T(8,128)} %constant.24.clone.table_ref) | copy-start | bytes 2752516
  40.7 0.6 copy-start.13
  50.4 0.9 copy-start.8
  51.3 0.9 copy-start.9
  52.2 9.2 %copy-start.14 = (f32[3,8,1024]{2,1,0:T(8,128)S(1)}, f32[3,8,1024]{2,1,0:T(8,128)}, u32[]{:S(2)}) copy-start(f32[3,8,1024]{2,1,0:T(8,128)} %copy-done.13) | copy-start | bytes 294916
  52.3 26.2 %copy-start.4 = (f32[4,2,128,128]{3,2,1,0:T(8,128)S(1)}, f32[4,2,128,128]{3,2,1,0:T(8,128)}, u32[]{:S(2)}) copy-start(f32[4,2,128,128]{3,2,1,0:T(8,128)} %constant.25.clone.twist_ref) | copy-start | bytes 1572868
  52.3 26.2 %copy-start.7 = (f32[4,128,128]{2,1,0:T(8,128)S(1)}, f32[4,128,128]{2,1,0:T(8,128)}, u32[]{:S(2)}) copy-start(f32[4,128,128]{2,1,0:T(8,128)} %constant.26.clone.last_ref) | copy-start | bytes 786436
  54.8 23.6 %all-to-all-start.1 = ((f32[128,1,384]{2,1,0:T(1,128)}), f32[128,1,384]{2,1,0:T(1,128)S(1)}, u32[]{:S(2)}, u32[]{:S(2)}) async-start(f32[128,1,384]{2,1,0:T(1,128)} %bitcast.12), calls=%async_computation.1 | async-start | bytes 393216 | tf_op jit(solution)/shard_map/all_to_all | solution.py:447
  61.5 14.1 %collective-permute-start.3 = (f32[3,8,1024]{2,1,0:T(8,128)S(1)}, f32[3,8,1024]{2,1,0:T(8,128)S(1)}, u32[]{:S(2)}, u32[]{:S(2)}) collective-permute-start(f32[3,8,1024]{2,1,0:T(8,128)S(1)} %copy-done.14), channel_id=1, source_target_pairs={{0,4},{4,8},{8,12},{12,16},{16,20},{20,24},{24,28},{28,32},{32,36}... | collective-permute-start | bytes 294920 | tf_op jit(solution)/shard_map/ppermute | solution.py:485
  64.0 11.7 %collective-permute-start.4 = (f32[3,8,1024]{2,1,0:T(8,128)S(1)}, f32[3,8,1024]{2,1,0:T(8,128)S(1)}, u32[]{:S(2)}, u32[]{:S(2)}) collective-permute-start(f32[3,8,1024]{2,1,0:T(8,128)S(1)} %copy-done.14), channel_id=1, source_target_pairs={{4,0},{8,4},{12,8},{16,12},{20,16},{24,20},{28,24},{32,28},{36,32}... | collective-permute-start | bytes 294920 | tf_op jit(solution)/shard_map/ppermute | solution.py:486
  79.4 4.9 %collective-permute-start.5 = (f32[2,2,8,1024]{3,2,1,0:T(8,128)S(1)}, f32[2,2,8,1024]{3,2,1,0:T(8,128)S(1)}, u32[]{:S(2)}, u32[]{:S(2)}) collective-permute-start(f32[2,2,8,1024]{3,2,1,0:T(8,128)S(1)} %get-tuple-element.12), channel_id=1, source_target_pairs={{0,1},{1,0},{2,3},{3,2},{4,5},{5,4},{6,7},{7,6},{8,9},{9,8},{10,11... | collective-permute-start | bytes 393224 | tf_op jit(solution)/shard_map/ppermute | solution.py:522
  84.3 6.1 %collective-permute-start.6 = (f32[2,8,1024]{2,1,0:T(8,128)S(1)}, f32[2,8,1024]{2,1,0:T(8,128)S(1)}, u32[]{:S(2)}, u32[]{:S(2)}) collective-permute-start(f32[2,8,1024]{2,1,0:T(8,128)S(1)} %fusion), channel_id=1, source_target_pairs={{0,2},{1,3},{2,0},{3,1},{4,6},{5,7},{6,4},{7,5},{8,10},{9,11},{10,... | collective-permute-start | bytes 196616 | tf_op jit(solution)/shard_map/ppermute | solution.py:523
where the time goes:
time: 91.5 us; the launch traced here: 91 us
  starting transfers between devices  56.2 us (61%)
  waiting for transfers between devices  15.6 us (17%)
  Pallas kernels  12.2 us (13%)
  local copies, waits for them, and re-layouts  5.28 us (6%)
  other arithmetic  1.63 us (2%)
    all_to_all x2, starting transfers between devices, all_to_all_x(): lax.all_to_all(shaped, 'gx', split_axis=0, concat_axis=0, tiled=True)  21.3 us
    pallas_call x6, Pallas kernels, call(): pl.pallas_call(body, out_shape=shapes, in_specs=specs, out_specs=jax.tree...  12.2 us
    ppermute x1, starting transfers between devices, local(): lax.ppermute(rows, 'gx', [((i + 1) % DEV_X, i) for i in range(DEV_X)])  9.31 us
    all_to_all x2, waiting for transfers between devices, all_to_all_x(): lax.all_to_all(shaped, 'gx', split_axis=0, concat_axis=0, tiled=True)  9.13 us
    ppermute x1, starting transfers between devices, local(): mate = lax.ppermute(own, 'gy', mate_pairs)  6.67 us
    unnamed x30, local copies, waits for them, and re-layouts  5.28 us
    ppermute x1, starting transfers between devices, local(): diagonal = lax.ppermute(far, 'gy', mate_pairs)  4.55 us
    ppermute x1, starting transfers between devices, local(): far = lax.ppermute(own, 'gy', far_pairs)  4.02 us
  transfers between devices with their start and end apart: 9, of which 6 were waited for; matrix products, arithmetic and copies ran while one was open for 0% of the time, Pallas kernels for 8%

commit v1 on v0

--- a/solution.py
+++ b/solution.py
@@ -3,6 +3,7 @@
 
 import jax
 import jax.numpy as jnp
+import ml_dtypes
 import numpy as np
 from jax import lax
 from jax.experimental import pallas as pl
@@ -14,7 +15,6 @@
 spacing = 0.1
 lift_height = 0.05
 area_weight = spacing * spacing
-highest = lax.Precision.HIGHEST
 
 ROWS = 8
 SPAN = 1024
@@ -30,6 +30,12 @@
 
 def real_form(coeff):
     return np.block([[coeff.real, -coeff.imag], [coeff.imag, coeff.real]])
+
+
+def halves(matrix):
+    high = matrix.astype(ml_dtypes.bfloat16).astype(np.float64)
+    low = (matrix - high).astype(ml_dtypes.bfloat16).astype(np.float64)
+    return np.stack([high, low]).astype(np.float32)
 
 
 def make_tables():
@@ -70,29 +76,41 @@
     col_back = real_form(grown.conj().T).T / (NX * NY)
     as32 = lambda x: np.asarray(x, np.float32)
     return {
-        "row_first": as32(np.stack(row_first)),
+        "row_first": np.stack([halves(x) for x in row_first]),
         "row_twist": as32(np.stack(row_twist)),
-        "outer": as32(outer),
+        "outer": halves(outer),
         "col_twist": as32(col_twist),
-        "col_small": as32(np.stack([col_small, col_back])),
+        "col_small": np.stack([halves(col_small), halves(col_back)]),
         "back_twist": as32(np.stack(back_twist)),
-        "back_last": as32(np.stack(back_last)),
+        "back_last": np.stack([halves(x) for x in back_last]),
     }
 
 
 TABLES = make_tables()
 
 
+def parts_of(x):
+    high = x.astype(jnp.bfloat16)
+    return high, (x - high.astype(jnp.float32)).astype(jnp.bfloat16)
+
+
+def product(left, right, dims):
+    def one(x, y):
+        return lax.dot_general(x, y, (dims, ((), ())), preferred_element_type=jnp.float32)
+
+    return one(left[0], right[0]) + (one(left[0], right[1]) + one(left[1], right[0]))
+
+
 def dot(left, right):
-    return lax.dot_general(
-        left, right, (((1,), (0,)), ((), ())), precision=highest, preferred_element_type=jnp.float32
-    )
+    return product(left, right, ((1,), (0,)))
 
 
 def dot_t(left, right):
-    return lax.dot_general(
-        left, right, (((1,), (1,)), ((), ())), precision=highest, preferred_element_type=jnp.float32
-    )
+    return product(left, right, ((1,), (1,)))
+
+
+def table_parts(ref):
+    return ref[0].astype(jnp.bfloat16), ref[1].astype(jnp.bfloat16)
 
 
 def tiles_of(cells):
@@ -140,7 +158,7 @@
             mate_real * mate[1] + mate_imag * mate[0]
         )
         stacked.append(jnp.concatenate([merged_real, merged_imag], 0))
-    stepped = dot(first, jnp.concatenate(stacked, 1))
+    stepped = dot(first, parts_of(jnp.concatenate(stacked, 1)))
     turned = []
     for b in range(3):
         part = stepped[:, LANES * b : LANES * (b + 1)]
@@ -156,7 +174,7 @@
                 0,
             )
         )
-    return dot_t(outer, jnp.concatenate(turned, 0))
+    return dot_t(outer, parts_of(jnp.concatenate(turned, 0)))
 
 
 def column_stage(blocks, kernels, outer, twist, small, small_back):
@@ -164,13 +182,14 @@
     minus_plus = half_sign(-1.0, 1.0)
     lower = [swap_halves(x, plus_minus) for x in blocks]
     stepped = dot(
-        outer, jnp.concatenate([jnp.concatenate(blocks, 1), jnp.concatenate(lower, 1)], 0)
+        outer,
+        parts_of(jnp.concatenate([jnp.concatenate(blocks, 1), jnp.concatenate(lower, 1)], 0)),
     )
     turned = []
     for b in range(3):
         part = stepped[:, LANES * b : LANES * (b + 1)]
         turned.append(part * twist[0] + pltpu.roll(part, 64, 1) * twist[1])
-    spectra = dot(jnp.concatenate(turned, 0), small)
+    spectra = dot(parts_of(jnp.concatenate(turned, 0)), small)
     plain = [spectra[LANES * b : LANES * (b + 1)] for b in range(3)]
     rolled = [pltpu.roll(x, 64, 1) for x in plain]
 
@@ -182,27 +201,30 @@
         times(1, 0) - 2.0 * times(2, 1),
         times(2, 0),
     ]
-    back = dot(jnp.concatenate(mixed, 0), small_back)
+    back = dot(parts_of(jnp.concatenate(mixed, 0)), small_back)
     upper, under = [], []
     for a in range(3):
         part = back[LANES * a : LANES * (a + 1)]
         turned = part * twist[0] - pltpu.roll(part, 64, 1) * twist[1]
         upper.append(turned)
         under.append(swap_halves(turned, minus_plus))
-    return dot(outer, jnp.concatenate([jnp.concatenate(upper, 1), jnp.concatenate(under, 1)], 0))
+    return dot(
+        outer, parts_of(jnp.concatenate([jnp.concatenate(upper, 1), jnp.concatenate(under, 1)], 0))
+    )
 
 
 def row_inverse(q, blocks, heights, outer, twist, last):
     minus_plus = half_sign(-1.0, 1.0)
     under = [swap_halves(x, minus_plus) for x in blocks]
     stepped = dot(
-        outer, jnp.concatenate([jnp.concatenate(blocks, 1), jnp.concatenate(under, 1)], 0)
+        outer,
+        parts_of(jnp.concatenate([jnp.concatenate(blocks, 1), jnp.concatenate(under, 1)], 0)),
     )
     turned = []
     for a in range(3):
         part = stepped[:, LANES * a : LANES * (a + 1)]
         turned.append(part * twist[0] + pltpu.roll(part, 64, 1) * twist[1])
-    fields = dot_t(last, jnp.concatenate(turned, 0))
+    fields = dot_t(last, parts_of(jnp.concatenate(turned, 0)))
     level = [fields[:, LANES * a : LANES * (a + 1)] for a in range(3)]
     sums = []
     for m, height in zip((0, 2, 1, 3), heights):
@@ -216,8 +238,12 @@
 vmem = pl.BlockSpec(memory_space=pltpu.VMEM)
 
 
-def call(body, shapes, *args, loose=0, scratch=(), flops=1_000_000, moved=1_000_000):
-    specs = [vmem] * (len(args) - loose) + [pl.BlockSpec(memory_space=pl.ANY)] * loose
+def call(body, shapes, *args, loose=0, waits=0, scratch=(), flops=1_000_000, moved=1_000_000):
+    blocks = len(args) - loose - waits
+    specs = [vmem] * blocks + [pl.BlockSpec(memory_space=pl.ANY)] * (loose + waits)
+    kept = list(args)
+    for n in range(blocks, blocks + loose):
+        kept[n] = pltpu.with_memory_space_constraint(jnp.asarray(args[n]), pltpu.HBM)
     return pl.pallas_call(
         body,
         out_shape=shapes,
@@ -226,26 +252,58 @@
         scratch_shapes=scratch,
         compiler_params=pltpu.CompilerParams(vmem_limit_bytes=40 * 1024 * 1024),
         cost_estimate=pl.CostEstimate(flops=flops, bytes_accessed=moved, transcendentals=0),
-    )(*args)
+    )(*kept)
+
+
+def held(*shape):
+    return pltpu.VMEM(shape, jnp.float32)
 
 
 def f32(*shape):
     return jax.ShapeDtypeStruct(shape, jnp.float32)
 
 
-def row_kernel(own_ref, far_ref, mate_ref, diag_ref, first_ref, twist_ref, outer_ref, out_ref):
+def fetch(pairs, sems):
+    copies = [pltpu.make_async_copy(src, dst, sems.at[n]) for n, (src, dst) in enumerate(pairs)]
+    for copy in copies:
+        copy.start()
+    return copies
+
+
+def pack_kernel(
+    unknown_ref, height_ref, first_ref, twist_ref, outer_ref, own_ref, first_out, twist_out, outer_out, sems
+):
+    q = lax.axis_index("gy")
+    copies = fetch(
+        [
+            (unknown_ref, own_ref.at[pl.ds(0, 2)]),
+            (height_ref, own_ref.at[2]),
+            (first_ref.at[q], first_out),
+            (twist_ref.at[q], twist_out),
+            (outer_ref, outer_out),
+        ],
+        sems,
+    )
+    for copy in copies:
+        copy.wait()
+
+
+def row_kernel(
+    own_ref, far_ref, mate_ref, diag_ref, first_ref, twist_ref, outer_ref, out_ref, low_ref
+):
     q = lax.axis_index("gy")
     blocks = [
         [tiles_of(ref[part]) for part in range(3)] for ref in (own_ref, far_ref, mate_ref, diag_ref)
     ]
-    out = row_spectra(q, blocks, first_ref[q], twist_ref[q], outer_ref[...])
+    out = row_spectra(q, blocks, table_parts(first_ref), twist_ref, table_parts(outer_ref))
     for b in range(3):
         out_ref[pl.ds(b, DEV_X, stride=3), :] = out[:, LANES * b : LANES * (b + 1)]
-
-
-def table_kernel(flat_ref, slope_ref, curve_ref, out_ref):
+    low_ref[...] = own_ref[:, TILE:]
+
+
+def spread_spectra(refs, out_ref):
     lane = lax.broadcasted_iota(jnp.int32, (64, LANES), 1)
-    for m, ref in enumerate((flat_ref, slope_ref, curve_ref)):
+    for m, ref in enumerate(refs):
         real = ref[pl.ds(0, 64, stride=2), :]
         imag = ref[pl.ds(1, 64, stride=2), :]
         for parity in range(2):
@@ -258,12 +316,22 @@
             )
 
 
-def column_kernel(in_ref, table_ref, outer_ref, twist_ref, small_ref, after_ref, out_ref):
+def column_kernel(
+    in_ref, spread_ref, outer_ref, twist_ref, small_ref, own_ref, after_ref, out_ref, high_ref
+):
     blocks = [in_ref[pl.ds(b, DEV_X, stride=3), :] for b in range(3)]
-    kernels = [(table_ref[2 * m], table_ref[2 * m + 1]) for m in range(3)]
-    out = column_stage(blocks, kernels, outer_ref[...], twist_ref, small_ref[0], small_ref[1])
+    kernels = [(spread_ref[2 * m], spread_ref[2 * m + 1]) for m in range(3)]
+    out = column_stage(
+        blocks,
+        kernels,
+        table_parts(outer_ref),
+        twist_ref,
+        table_parts(small_ref.at[0]),
+        table_parts(small_ref.at[1]),
+    )
     for a in range(3):
         out_ref[pl.ds(a, DEV_X, stride=3), :] = out[:, LANES * a : LANES * (a + 1)]
+    high_ref[...] = own_ref[:, :TILE]
 
 
 def inverse_kernel(
@@ -275,15 +343,17 @@
     outer_ref,
     twist_ref,
     last_ref,
-    after_ref,
+    down_ref,
     same_ref,
-    mate_out_ref,
+    crossed_ref,
 ):
     q = lax.axis_index("gy")
     blocks = [in_ref[pl.ds(a, DEV_X, stride=3), :] for a in range(3)]
     heights = [tiles_of(ref[2]) for ref in (own_ref, far_ref, mate_ref, diag_ref)]
-    sums = row_inverse(q, blocks, heights, outer_ref[...], twist_ref[q], last_ref[q])
-    places = ((same_ref, 0), (same_ref, 1), (mate_out_ref, 0), (mate_out_ref, 1))
+    sums = row_inverse(
+        q, blocks, heights, table_parts(outer_ref), twist_ref, table_parts(last_ref)
+    )
+    places = ((same_ref, 0), (same_ref, 1), (crossed_ref, 0), (crossed_ref, 1))
     for (ref, slot), pair in zip(places, sums):
         for part in range(2):
             for n in range(SUBS):
@@ -302,11 +372,8 @@
     return [float(c) for c in moved.coef[::-1]]
 
 
-COS_FIT = fit(lambda x: np.cos(wave_number * np.sqrt(x)), 10)
-SIN_FIT = fit(
-    lambda x: wave_number * np.sinc(2.0 * np.sqrt(x)),
-    9,
-)
+COS_FIT = fit(lambda x: np.cos(wave_number * np.sqrt(x)), 9)
+SIN_FIT = fit(lambda x: wave_number * np.sinc(2.0 * np.sqrt(x)), 8)
 
 
 def near_table(kinds):
@@ -328,7 +395,10 @@
                 k2 = 0.5 * (second_r * rise**2 + first_r * (1 - rise**2) / radius)
                 a0 = green - lift_height * k1 + lift_height**2 * k2
                 a1 = k1 - 2 * lift_height * k2
-                entry = [rho2, a0.real, a1.real, k2.real, a0.imag, a1.imag, k2.imag]
+                offset = rho2 - X_TOP / 2
+                line = SIN_FIT[-2] - k2.imag
+                level = SIN_FIT[-1] - a0.imag + k2.imag * offset
+                entry = [offset, a0.real, a1.real, k2.real, level, line, a1.imag]
                 entries.append([np.tile(e, (ROWS // TILE, LANES // TILE)) for e in entry])
     return np.asarray(entries, np.float32)
 
@@ -362,15 +432,13 @@
     real, imag, height = source
     w = raised - height
     v = w * w
-    x = v + table_ref[entry, 0]
-    u = x - X_TOP / 2
-    root = lax.rsqrt(x)
+    u = v + table_ref[entry, 0]
+    root = lax.rsqrt(u + X_TOP / 2)
     gap_real = horner(COS_FIT, u) * root - (
         table_ref[entry, 2] * w + (table_ref[entry, 3] * v + table_ref[entry, 1])
     )
-    gap_imag = horner(SIN_FIT, u) - (
-        table_ref[entry, 5] * w + (table_ref[entry, 6] * v + table_ref[entry, 4])
-    )
+    fitted = (horner(SIN_FIT[:-2], u) * u + table_ref[entry, 5]) * u + table_ref[entry, 4]
+    gap_imag = fitted - table_ref[entry, 6] * w
     return gap_real * real - gap_imag * imag, gap_real * imag + gap_imag * real
 
 
@@ -389,8 +457,53 @@
     return total_real, total_imag
 
 
-def side_kernel(own_ref, far_ref, mate_ref, diag_ref, table_ref, after_ref, out_ref, rows_ref, edge):
+def spread_kernel(
+    flat_ref,
+    slope_ref,
+    curve_ref,
+    twist_ref,
+    small_ref,
+    after_ref,
+    spread_ref,
+    twist_out,
+    small_out,
+    lined,
+    sems,
+):
+    copies = fetch(
+        [
+            (flat_ref, lined.at[0]),
+            (slope_ref, lined.at[1]),
+            (curve_ref, lined.at[2]),
+            (twist_ref, twist_out),
+            (small_ref, small_out),
+        ],
+        sems,
+    )
+    for copy in copies:
+        copy.wait()
+    spread_spectra([lined.at[m] for m in range(3)], spread_ref)
+
+
+def side_kernel(
+    own_ref,
+    far_ref,
+    mate_ref,
+    diag_ref,
+    table_ref,
+    back_twist_ref,
+    back_last_ref,
+    after_ref,
+    out_ref,
+    back_twist_out,
+    back_last_out,
+    edge,
+    sems,
+):
     q = lax.axis_index("gy")
+    copies = fetch(
+        [(back_twist_ref.at[q], back_twist_out), (back_last_ref.at[q], back_last_out)], sems
+    )
     odd = q % 2 == 1
     for part in range(3):
         last = slice(SPAN - LANES, SPAN)
@@ -399,7 +512,6 @@
         edge[SUBS + 1, part] = jnp.where(odd, diag_ref[part, :, first], mate_ref[part, :, first])
         for n in range(SUBS):
             edge[n + 1, part] = own_ref[part, :, LANES * n : LANES * (n + 1)]
-    rows_ref[...] = own_ref[...]
     lane = lax.broadcasted_iota(jnp.int32, (ROWS, LANES), 1)
 
     for n in range(SUBS):
@@ -421,25 +533,24 @@
         real, imag = meet_tiles(here[2] + lift_height, (here, left, right), table_ref)
         out_ref[0, :, LANES * n : LANES * (n + 1)] = area_weight * real
         out_ref[1, :, LANES * n : LANES * (n + 1)] = area_weight * imag
-
-
-def over_kernel(own_ref, up_ref, down_ref, table_ref, side_ref, after_ref, out_ref):
-    sub = lax.broadcasted_iota(jnp.int32, (ROWS, LANES), 0)
+    for copy in copies:
+        copy.wait()
+
+
+def over_kernel(own_ref, up_ref, down_ref, table_ref, side_ref, same_ref, mate_ref, out_ref):
     for n in range(SUBS):
         lanes = slice(LANES * n, LANES * (n + 1))
         here = [own_ref[part, :, lanes] for part in range(3)]
-        swapped = [pltpu.roll(x, TILE, 0) for x in here]
         above = [
-            jnp.where(sub < TILE, pltpu.roll(up_ref[part, :, lanes], TILE, 0), swapped[part])
-            for part in range(3)
+            jnp.concatenate([up_ref[part, :, lanes], here[part][:TILE]], 0) for part in range(3)
         ]
         below = [
-            jnp.where(sub < TILE, swapped[part], pltpu.roll(down_ref[part, :, lanes], TILE, 0))
-            for part in range(3)
+            jnp.concatenate([here[part][TILE:], down_ref[part, :, lanes]], 0) for part in range(3)
         ]
         real, imag = meet_tiles(here[2] + lift_height, (above, below), table_ref)
-        out_ref[0, :, lanes] = side_ref[0, :, lanes] + area_weight * real
-        out_ref[1, :, lanes] = side_ref[1, :, lanes] + area_weight * imag
+        for part, near in enumerate((real, imag)):
+            spectral = same_ref[0, part, :, lanes] + mate_ref[0, part, :, lanes]
+            out_ref[part, :, lanes] = spectral + (side_ref[part, :, lanes] + area_weight * near)
 
 
 def all_to_all_x(messages):
@@ -451,52 +562,103 @@
 def local(unknown, height, spectrum_flat, spectrum_slope, spectrum_curve):
     mate_pairs = [(g, g ^ 1) for g in range(DEV_Y)]
     far_pairs = [(g, g ^ 2) for g in range(DEV_Y)]
-    own = jnp.concatenate([unknown, height[None]], 0)
+    own, row_first, row_twist, outer = call(
+        pack_kernel,
+        (
+            f32(3, ROWS, SPAN),
+            held(2, LANES, LANES),
+            held(2, HALF, LANES),
+            held(2, LANES, 2 * LANES),
+        ),
+        unknown,
+        height,
+        TABLES["row_first"],
+        TABLES["row_twist"],
+        TABLES["outer"],
+        loose=5,
+        scratch=[pltpu.SemaphoreType.DMA((5,))],
+    )
     far = lax.ppermute(own, "gy", far_pairs)
     mate = lax.ppermute(own, "gy", mate_pairs)
     diagonal = lax.ppermute(far, "gy", mate_pairs)
     groups = (own, far, mate, diagonal)
-
+    sent, low = call(
+        row_kernel,
+        (f32(3 * DEV_X, LANES), f32(3, TILE, SPAN)),
+        *groups,
+        row_first,
+        row_twist,
+        outer,
+    )
+    arrived = all_to_all_x(sent)
     lined = [
         s.reshape(2, 64, LANES).transpose(1, 0, 2).reshape(2 * 64, LANES)
         for s in (spectrum_flat, spectrum_slope, spectrum_curve)
     ]
-    table = call(table_kernel, f32(6, LANES, LANES), *lined)
-
-    sent = call(
-        row_kernel,
-        f32(3 * DEV_X, LANES),
-        *groups,
-        TABLES["row_first"],
-        TABLES["row_twist"],
-        TABLES["outer"],
-    )
-    arrived = all_to_all_x(sent)
-    side, rows = call(
+    spread, col_twist, col_small = call(
+        spread_kernel,
+        (
+            held(6, LANES, LANES),
+            held(2, LANES, LANES),
+            held(2, 2, LANES, LANES),
+        ),
+        *lined,
+        TABLES["col_twist"],
+        TABLES["col_small"],
+        sent,
+        loose=5,
+        waits=1,
+        scratch=[
+            pltpu.VMEM((3, LANES, LANES), jnp.float32),
+            pltpu.SemaphoreType.DMA((5,)),
+        ],
+        flops=10_000_000,
+    )
+    up = lax.ppermute(low, "gx", [(i, (i + 1) % DEV_X) for i in range(DEV_X)])
+    back, high = call(
+        column_kernel,
+        (f32(3 * DEV_X, LANES), f32(3, TILE, SPAN)),
+        arrived,
+        spread,
+        outer,
+        col_twist,
+        col_small,
+        own,
+        up,
+        waits=1,
+    )
+    down = lax.ppermute(high, "gx", [((i + 1) % DEV_X, i) for i in range(DEV_X)])
+    returned = all_to_all_x(back)
+    side, back_twist, back_last = call(
         side_kernel,
-        (f32(2, ROWS, SPAN), f32(3, ROWS, SPAN)),
+        (held(2, ROWS, SPAN), held(2, LANES, LANES), held(2, LANES, LANES)),
         *groups,
         SIDE_TABLE,
-        sent,
-        loose=1,
-        scratch=[pltpu.VMEM((SUBS + 2, 3, ROWS, LANES), jnp.float32)],
+        TABLES["back_twist"],
+        TABLES["back_last"],
+        back,
+        loose=2,
+        waits=1,
+        scratch=[
+            pltpu.VMEM((SUBS + 2, 3, ROWS, LANES), jnp.float32),
+            pltpu.SemaphoreType.DMA((2,)),
+        ],
         flops=30_000_000,
     )
-    up = lax.ppermute(rows, "gx", [(i, (i + 1) % DEV_X) for i in range(DEV_X)])
-    down = lax.ppermute(rows, "gx", [((i + 1) % DEV_X, i) for i in range(DEV_X)])
-    back = call(
-        column_kernel,
-        f32(3 * DEV_X, LANES),
-        arrived,
-        table,
-        TABLES["outer"],
-        TABLES["col_twist"],
-        TABLES["col_small"],
-        side,
-        loose=1,
-    )
-    returned = all_to_all_x(back)
-    near = call(
+    same, crossed = call(
+        inverse_kernel,
+        (f32(2, 2, ROWS, SPAN), f32(2, 2, ROWS, SPAN)),
+        returned,
+        *groups,
+        outer,
+        back_twist,
+        back_last,
+        down,
+        waits=1,
+    )
+    from_mate = lax.ppermute(crossed, "gy", mate_pairs)
+    from_far = lax.ppermute(same[1] + from_mate[1], "gy", far_pairs)
+    base = call(
         over_kernel,
         f32(2, ROWS, SPAN),
         own,
@@ -504,24 +666,11 @@
         down,
         OVER_TABLE,
         side,
-        back,
-        loose=1,
+        same,
+        from_mate,
         flops=20_000_000,
     )
-    same, crossed = call(
-        inverse_kernel,
-        (f32(2, 2, ROWS, SPAN), f32(2, 2, ROWS, SPAN)),
-        returned,
-        *groups,
-        TABLES["outer"],
-        TABLES["back_twist"],
-        TABLES["back_last"],
-        near,
-        loose=1,
-    )
-    from_mate = lax.ppermute(crossed, "gy", mate_pairs)
-    from_far = lax.ppermute(same[1] + from_mate[1], "gy", far_pairs)
-    return (same[0] + from_mate[0] + near) + from_far
+    return base + from_far
 
 
 def solution(mesh):

time: 91.5 us -> 83.2 us (0.909)
  local copies, waits for them, and re-layouts: 5.28 us -> 0.01 us
  waiting for transfers between devices: 15.6 us -> 13 us
  starting transfers between devices: 56.2 us -> 57.2 us
  other arithmetic: 1.63 us -> 0.65 us
    all_to_all x2, waiting for transfers between devices: 9.13 us -> 1.44 us  [all_to_all_x(): lax.all_to_all(shaped, 'gx', split_axis=0, concat_axis=0, tiled=True)]
    ppermute x2, waiting for transfers between devices: 2.38 us -> 9.28 us  [the longest x1 9.28 us: local(): up = lax.ppermute(low, 'gx', [(i, (i + 1) % DEV_X) for i in range(DEV_X)])]
    unnamed x30 -> x4, local copies, waits for them, and re-layouts: 5.28 us -> 0.01 us
    ppermute x1, waiting for transfers between devices: 2.16 us -> 0.4 us  [local(): from_far = lax.ppermute(same[1] + from_mate[1], 'gy', far_pairs)]
    ppermute x1, starting transfers between devices: 3.9 us -> 5.36 us  [local(): from_mate = lax.ppermute(crossed, 'gy', mate_pairs)]
    ppermute x1, starting transfers between devices: 3.91 us -> 2.54 us  [local(): from_far = lax.ppermute(same[1] + from_mate[1], 'gy', far_pairs)]
    concatenate x1 -> x0, other arithmetic: 0.97 us -> none  [local(): own = jnp.concatenate([unknown, height[None]], 0)]
    pallas_call x6 -> x7, Pallas kernels: 12.2 us -> 11.7 us  [call(): pl.pallas_call(body, out_shape=shapes, in_specs=specs, out_specs=jax.tree...]
where the time goes in v1:
time: 83.2 us; the launch traced here: 82.8 us
  starting transfers between devices  57.2 us (69%)
  waiting for transfers between devices  13 us (16%)
  Pallas kernels  11.7 us (14%)
    all_to_all x2, starting transfers between devices, all_to_all_x(): lax.all_to_all(shaped, 'gx', split_axis=0, concat_axis=0, tiled=True)  21.9 us
    pallas_call x7, Pallas kernels, call(): pl.pallas_call(body, out_shape=shapes, in_specs=specs, out_specs=jax.tree...  11.7 us
    ppermute x1, starting transfers between devices, local(): lax.ppermute(high, 'gx', [((i + 1) % DEV_X, i) for i in range(DEV_X)])  9.56 us
    ppermute x1, waiting for transfers between devices, local(): up = lax.ppermute(low, 'gx', [(i, (i + 1) % DEV_X) for i in range(DEV_X)])  9.28 us
    ppermute x1, starting transfers between devices, local(): mate = lax.ppermute(own, 'gy', mate_pairs)  6.67 us
    ppermute x1, starting transfers between devices, local(): from_mate = lax.ppermute(crossed, 'gy', mate_pairs)  5.36 us
    ppermute x1, starting transfers between devices, local(): diagonal = lax.ppermute(far, 'gy', mate_pairs)  4.55 us
    ppermute x1, starting transfers between devices, local(): far = lax.ppermute(own, 'gy', far_pairs)  4.03 us
  transfers between devices with their start and end apart: 9, of which 6 were waited for; matrix products, arithmetic and copies ran while one was open for 0% of the time, Pallas kernels for 8%

profile of v1, /device:TPU:1, one launch (start us, length us, event | category | flops | bytes accessed | tf_op | source)
XLA Modules:
  0.0 82.8 jit_solution(8698604188416197189)
XLA Ops:
  0.0 1.1 %shard_map.136 = (f32[3,8,1024]{2,1,0:T(8,128)S(1)}, f32[2,128,128]{2,1,0:T(8,128)S(1)}, f32[2,64,128]{2,1,0:T(8,128)S(1)}, f32[2,128,256]{2,1,0:T(8,128)S(1)}) custom-call(f32[2,8,1024]{2,1,0:T(8,128)} %unknown_ref.1, f32[8,1024]{1,0:T(8,128)} %height_ref.1, f32[4,2,128,128]{3,2,1,0:T(8,128)} %constant.18.clone.first_ref, ...), custom_call_target="tpu_custom_call" | custom-call | flops 1000000 | bytes 1000000 | tf_op jit(solution)/shard_map/pallas_call | solution.py:247
  1.2 4.0 %collective-permute-start = (f32[3,8,1024]{2,1,0:T(8,128)S(1)}, f32[3,8,1024]{2,1,0:T(8,128)S(1)}, u32[]{:S(2)}, u32[]{:S(2)}) collective-permute-start(f32[3,8,1024]{2,1,0:T(8,128)S(1)} %get-tuple-element.21.own_ref), channel_id=1, source_target_pairs={{0,2},{1,3},{2,0},{3,1},{4,6},{5,7},{6,4},{7,5},{8,10},{9,11},{10,... | collective-permute-start | bytes 294920 | tf_op jit(solution)/shard_map/ppermute | solution.py:581
  5.2 6.7 %collective-permute-start.1 = (f32[3,8,1024]{2,1,0:T(8,128)S(1)}, f32[3,8,1024]{2,1,0:T(8,128)S(1)}, u32[]{:S(2)}, u32[]{:S(2)}) collective-permute-start(f32[3,8,1024]{2,1,0:T(8,128)S(1)} %get-tuple-element.21.own_ref), channel_id=1, source_target_pairs={{0,1},{1,0},{2,3},{3,2},{4,5},{5,4},{6,7},{7,6},{8,9},{9,8},{10,11... | collective-permute-start | bytes 294920 | tf_op jit(solution)/shard_map/ppermute | solution.py:582
  11.9 0.0 collective-permute-done.far_ref
  11.9 4.6 %collective-permute-start.2 = (f32[3,8,1024]{2,1,0:T(8,128)S(1)}, f32[3,8,1024]{2,1,0:T(8,128)S(1)}, u32[]{:S(2)}, u32[]{:S(2)}) collective-permute-start(f32[3,8,1024]{2,1,0:T(8,128)S(1)} %collective-permute-done.far_ref), channel_id=1, source_target_pairs={{0,1},{1,0},{2,3},{3,2},{4,5},{5,4},{6,7},{7,6},{8,9},{9,8},{10,11... | collective-permute-start | bytes 294920 | tf_op jit(solution)/shard_map/ppermute | solution.py:583
  16.4 0.0 collective-permute-done.1.mate_ref
  16.5 0.9 %collective-permute-done.2.diag_ref = f32[3,8,1024]{2,1,0:T(8,128)S(1)} collective-permute-done((f32[3,8,1024]{2,1,0:T(8,128)S(1)}, f32[3,8,1024]{2,1,0:T(8,128)S(1)}, u32[]{:S(2)}, u32[]{:S(2)}) %collective-permute-start.2) | collective-permute-done | bytes 98336 | tf_op jit(solution)/shard_map/ppermute | solution.py:583
  17.4 1.4 %shard_map.137 = (f32[384,128]{1,0:T(8,128)}, f32[3,4,1024]{2,1,0:T(4,128)S(1)}) custom-call(f32[3,8,1024]{2,1,0:T(8,128)S(1)} %get-tuple-element.21.own_ref, f32[3,8,1024]{2,1,0:T(8,128)S(1)} %collective-permute-done.far_ref, f32[3,8,1024]{2,1,0:T(8,128)S(1)} %collective-permute-done.1.mate_ref, f32[3,8,1024]{2,1,0:T(8,128)S(1)} %collective-permute-done.2.diag_ref, ...), custom_call_target="tpu_custom_call" | custom-call | flops 1000000 | bytes 1000000 | tf_op jit(solution)/shard_map/pallas_call | solution.py:247
  18.8 14.6 %all-to-all-start = ((f32[128,1,384]{2,1,0:T(1,128)}), f32[128,1,384]{2,1,0:T(1,128)S(1)}, u32[]{:S(2)}, u32[]{:S(2)}) async-start(f32[128,1,384]{2,1,0:T(1,128)} %bitcast), calls=%async_computation | async-start | bytes 393216 | tf_op jit(solution)/shard_map/all_to_all | solution.py:558
  33.4 0.0 copy-start
  33.4 2.6 %collective-permute-start.3 = (f32[3,4,1024]{2,1,0:T(4,128)S(1)}, f32[3,4,1024]{2,1,0:T(4,128)S(1)}, u32[]{:S(2)}, u32[]{:S(2)}) collective-permute-start(f32[3,4,1024]{2,1,0:T(4,128)S(1)} %get-tuple-element.25), channel_id=1, source_target_pairs={{0,4},{4,8},{8,12},{12,16},{16,20},{20,24},{24,28},{28,32},{32,36}... | collective-permute-start | bytes 147464 | tf_op jit(solution)/shard_map/ppermute | solution.py:617
  36.0 1.3 %shard_map.138 = (f32[6,128,128]{2,1,0:T(8,128)S(1)}, f32[2,128,128]{2,1,0:T(8,128)S(1)}, f32[2,2,128,128]{3,2,1,0:T(8,128)S(1)}) custom-call(f32[128,128]{1,0:T(8,128)} %bitcast.23, f32[128,128]{1,0:T(8,128)} %bitcast.24, f32[128,128]{1,0:T(8,128)} %bitcast.25, f32[2,128,128]{2,1,0:T(8,128)} %constant.21.clone.twist_ref, ...), custom_call_target="tpu_custom_call" | custom-call | flops 10000000 | bytes 1000000 | tf_op jit(solution)/shard_map/pallas_call | solution.py:247
  37.3 9.3 %collective-permute-done.3.after_ref.up_ref = f32[3,4,1024]{2,1,0:T(4,128)S(1)} collective-permute-done((f32[3,4,1024]{2,1,0:T(4,128)S(1)}, f32[3,4,1024]{2,1,0:T(4,128)S(1)}, u32[]{:S(2)}, u32[]{:S(2)}) %collective-permute-start.3) | collective-permute-done | bytes 49184 | tf_op jit(solution)/shard_map/ppermute | solution.py:617
  46.6 1.0 %all-to-all-done = f32[128,1,384]{2,1,0:T(1,128)S(1)} async-done(((f32[128,1,384]{2,1,0:T(1,128)}), f32[128,1,384]{2,1,0:T(1,128)S(1)}, u32[]{:S(2)}, u32[]{:S(2)}) %all-to-all-start) | async-done | bytes 196640 | tf_op jit(solution)/shard_map/all_to_all | solution.py:558
  47.6 2.0 %shard_map.139 = (f32[384,128]{1,0:T(8,128)}, f32[3,4,1024]{2,1,0:T(4,128)S(1)}) custom-call(f32[384,128]{1,0:T(8,128)S(1)} %bitcast.22, f32[6,128,128]{2,1,0:T(8,128)S(1)} %get-tuple-element.27.spread_ref, f32[2,128,256]{2,1,0:T(8,128)S(1)} %get-tuple-element.24.outer_ref, f32[2,128,128]{2,1,0:T(8,128)S(1)} %get-tuple-element.28.twist_ref, ...), custom_call_target="tpu_custom_call" | custom-call | flops 1000000 | bytes 1000000 | tf_op jit(solution)/shard_map/pallas_call | solution.py:247
  49.7 7.3 %all-to-all-start.1 = ((f32[128,1,384]{2,1,0:T(1,128)}), f32[128,1,384]{2,1,0:T(1,128)S(1)}, u32[]{:S(2)}, u32[]{:S(2)}) async-start(f32[128,1,384]{2,1,0:T(1,128)} %bitcast.11), calls=%async_computation.1 | async-start | bytes 393216 | tf_op jit(solution)/shard_map/all_to_all | solution.py:558
  57.0 9.6 %collective-permute-start.4 = (f32[3,4,1024]{2,1,0:T(4,128)S(1)}, f32[3,4,1024]{2,1,0:T(4,128)S(1)}, u32[]{:S(2)}, u32[]{:S(2)}) collective-permute-start(f32[3,4,1024]{2,1,0:T(4,128)S(1)} %get-tuple-element.30), channel_id=1, source_target_pairs={{4,0},{8,4},{12,8},{16,12},{20,16},{24,20},{28,24},{32,28},{36,32}... | collective-permute-start | bytes 147464 | tf_op jit(solution)/shard_map/ppermute | solution.py:630
  66.5 0.0 copy-done
  66.5 3.1 %shard_map.140 = (f32[2,8,1024]{2,1,0:T(8,128)S(1)}, f32[2,128,128]{2,1,0:T(8,128)S(1)}, f32[2,128,128]{2,1,0:T(8,128)S(1)}) custom-call(f32[3,8,1024]{2,1,0:T(8,128)S(1)} %get-tuple-element.21.own_ref, f32[3,8,1024]{2,1,0:T(8,128)S(1)} %collective-permute-done.far_ref, f32[3,8,1024]{2,1,0:T(8,128)S(1)} %collective-permute-done.1.mate_ref, ...), custom_call_target="tpu_custom_call" | custom-call | flops 30000000 | bytes 1000000 | tf_op jit(solution)/shard_map/pallas_call | solution.py:247
  69.7 0.0 copy-start.1
  69.7 0.0 collective-permute-done.4.down_ref
  69.7 0.4 all-to-all-done.1
  70.1 0.7 shard_map.141
  70.8 5.4 %collective-permute-start.5 = (f32[2,2,8,1024]{3,2,1,0:T(8,128)S(1)}, f32[2,2,8,1024]{3,2,1,0:T(8,128)S(1)}, u32[]{:S(2)}, u32[]{:S(2)}) collective-permute-start(f32[2,2,8,1024]{3,2,1,0:T(8,128)S(1)} %get-tuple-element.36), channel_id=1, source_target_pairs={{0,1},{1,0},{2,3},{3,2},{4,5},{5,4},{6,7},{7,6},{8,9},{9,8},{10,11... | collective-permute-start | bytes 393224 | tf_op jit(solution)/shard_map/ppermute | solution.py:659
  76.2 1.0 %collective-permute-done.5.mate_ref = f32[2,2,8,1024]{3,2,1,0:T(8,128)S(1)} collective-permute-done((f32[2,2,8,1024]{3,2,1,0:T(8,128)S(1)}, f32[2,2,8,1024]{3,2,1,0:T(8,128)S(1)}, u32[]{:S(2)}, u32[]{:S(2)}) %collective-permute-start.5) | collective-permute-done | bytes 131104 | tf_op jit(solution)/shard_map/ppermute | solution.py:659
  77.1 2.5 %collective-permute-start.6 = (f32[2,8,1024]{2,1,0:T(8,128)S(1)}, f32[2,8,1024]{2,1,0:T(8,128)S(1)}, u32[]{:S(2)}, u32[]{:S(2)}) collective-permute-start(f32[2,8,1024]{2,1,0:T(8,128)S(1)} %fusion), channel_id=1, source_target_pairs={{0,2},{1,3},{2,0},{3,1},{4,6},{5,7},{6,4},{7,5},{8,10},{9,11},{10,... | collective-permute-start | bytes 196616 | tf_op jit(solution)/shard_map/ppermute | solution.py:660
  79.7 0.0 copy-done.1
  79.7 2.0 %shard_map.142 = f32[2,8,1024]{2,1,0:T(8,128)S(1)} custom-call(f32[3,8,1024]{2,1,0:T(8,128)S(1)} %get-tuple-element.21.own_ref, f32[3,4,1024]{2,1,0:T(4,128)S(1)} %collective-permute-done.3.after_ref.up_ref, f32[3,4,1024]{2,1,0:T(4,128)S(1)} %collective-permute-done.4.down_ref, f32[32,7,8,128]{3,2,1,0:T(8,128)S(1)} %copy-done.1, ...), custom_call_target="tpu_custom_call" | custom-call | flops 20000000 | bytes 1000000 | tf_op jit(solution)/shard_map/pallas_call | solution.py:247
  81.8 0.4 collective-permute-done.6
  82.2 0.6 add.11
  (1 shorter events, 0.0 us)
Async XLA Ops:
  1.2 10.7 %collective-permute-start = (f32[3,8,1024]{2,1,0:T(8,128)S(1)}, f32[3,8,1024]{2,1,0:T(8,128)S(1)}, u32[]{:S(2)}, u32[]{:S(2)}) collective-permute-start(f32[3,8,1024]{2,1,0:T(8,128)S(1)} %get-tuple-element.21.own_ref), channel_id=1, source_target_pairs={{0,2},{1,3},{2,0},{3,1},{4,6},{5,7},{6,4},{7,5},{8,10},{9,11},{10,... | collective-permute-start | bytes 294920 | tf_op jit(solution)/shard_map/ppermute | solution.py:581
  5.2 11.3 %collective-permute-start.1 = (f32[3,8,1024]{2,1,0:T(8,128)S(1)}, f32[3,8,1024]{2,1,0:T(8,128)S(1)}, u32[]{:S(2)}, u32[]{:S(2)}) collective-permute-start(f32[3,8,1024]{2,1,0:T(8,128)S(1)} %get-tuple-element.21.own_ref), channel_id=1, source_target_pairs={{0,1},{1,0},{2,3},{3,2},{4,5},{5,4},{6,7},{7,6},{8,9},{9,8},{10,11... | collective-permute-start | bytes 294920 | tf_op jit(solution)/shard_map/ppermute | solution.py:582
  11.9 5.5 %collective-permute-start.2 = (f32[3,8,1024]{2,1,0:T(8,128)S(1)}, f32[3,8,1024]{2,1,0:T(8,128)S(1)}, u32[]{:S(2)}, u32[]{:S(2)}) collective-permute-start(f32[3,8,1024]{2,1,0:T(8,128)S(1)} %collective-permute-done.far_ref), channel_id=1, source_target_pairs={{0,1},{1,0},{2,3},{3,2},{4,5},{5,4},{6,7},{7,6},{8,9},{9,8},{10,11... | collective-permute-start | bytes 294920 | tf_op jit(solution)/shard_map/ppermute | solution.py:583
  18.8 28.9 %all-to-all-start = ((f32[128,1,384]{2,1,0:T(1,128)}), f32[128,1,384]{2,1,0:T(1,128)S(1)}, u32[]{:S(2)}, u32[]{:S(2)}) async-start(f32[128,1,384]{2,1,0:T(1,128)} %bitcast), calls=%async_computation | async-start | bytes 393216 | tf_op jit(solution)/shard_map/all_to_all | solution.py:558
  33.4 33.1 %copy-start = (f32[48,7,8,128]{3,2,1,0:T(8,128)S(1)}, f32[48,7,8,128]{3,2,1,0:T(8,128)}, u32[]{:S(2)}) copy-start(f32[48,7,8,128]{3,2,1,0:T(8,128)} %constant.25.clone.table_ref) | copy-start | bytes 4128772
  33.4 13.2 %collective-permute-start.3 = (f32[3,4,1024]{2,1,0:T(4,128)S(1)}, f32[3,4,1024]{2,1,0:T(4,128)S(1)}, u32[]{:S(2)}, u32[]{:S(2)}) collective-permute-start(f32[3,4,1024]{2,1,0:T(4,128)S(1)} %get-tuple-element.25), channel_id=1, source_target_pairs={{0,4},{4,8},{8,12},{12,16},{16,20},{20,24},{24,28},{28,32},{32,36}... | collective-permute-start | bytes 147464 | tf_op jit(solution)/shard_map/ppermute | solution.py:617
  49.7 20.4 %all-to-all-start.1 = ((f32[128,1,384]{2,1,0:T(1,128)}), f32[128,1,384]{2,1,0:T(1,128)S(1)}, u32[]{:S(2)}, u32[]{:S(2)}) async-start(f32[128,1,384]{2,1,0:T(1,128)} %bitcast.11), calls=%async_computation.1 | async-start | bytes 393216 | tf_op jit(solution)/shard_map/all_to_all | solution.py:558
  57.0 12.7 %collective-permute-start.4 = (f32[3,4,1024]{2,1,0:T(4,128)S(1)}, f32[3,4,1024]{2,1,0:T(4,128)S(1)}, u32[]{:S(2)}, u32[]{:S(2)}) collective-permute-start(f32[3,4,1024]{2,1,0:T(4,128)S(1)} %get-tuple-element.30), channel_id=1, source_target_pairs={{4,0},{8,4},{12,8},{16,12},{20,16},{24,20},{28,24},{32,28},{36,32}... | collective-permute-start | bytes 147464 | tf_op jit(solution)/shard_map/ppermute | solution.py:630
  69.7 10.0 %copy-start.1 = (f32[32,7,8,128]{3,2,1,0:T(8,128)S(1)}, f32[32,7,8,128]{3,2,1,0:T(8,128)}, u32[]{:S(2)}) copy-start(f32[32,7,8,128]{3,2,1,0:T(8,128)} %constant.26.clone.table_ref) | copy-start | bytes 2752516
  70.8 6.3 %collective-permute-start.5 = (f32[2,2,8,1024]{3,2,1,0:T(8,128)S(1)}, f32[2,2,8,1024]{3,2,1,0:T(8,128)S(1)}, u32[]{:S(2)}, u32[]{:S(2)}) collective-permute-start(f32[2,2,8,1024]{3,2,1,0:T(8,128)S(1)} %get-tuple-element.36), channel_id=1, source_target_pairs={{0,1},{1,0},{2,3},{3,2},{4,5},{5,4},{6,7},{7,6},{8,9},{9,8},{10,11... | collective-permute-start | bytes 393224 | tf_op jit(solution)/shard_map/ppermute | solution.py:659
  77.1 5.0 %collective-permute-start.6 = (f32[2,8,1024]{2,1,0:T(8,128)S(1)}, f32[2,8,1024]{2,1,0:T(8,128)S(1)}, u32[]{:S(2)}, u32[]{:S(2)}) collective-permute-start(f32[2,8,1024]{2,1,0:T(8,128)S(1)} %fusion), channel_id=1, source_target_pairs={{0,2},{1,3},{2,0},{3,1},{4,6},{5,7},{6,4},{7,5},{8,10},{9,11},{10,... | collective-permute-start | bytes 196616 | tf_op jit(solution)/shard_map/ppermute | solution.py:660

commit v2 on v1

--- a/solution.py
+++ b/solution.py
@@ -317,7 +317,7 @@
 
 
 def column_kernel(
-    in_ref, spread_ref, outer_ref, twist_ref, small_ref, own_ref, after_ref, out_ref, high_ref
+    in_ref, spread_ref, outer_ref, twist_ref, small_ref, own_ref, side_ref, out_ref, high_ref
 ):
     blocks = [in_ref[pl.ds(b, DEV_X, stride=3), :] for b in range(3)]
     kernels = [(spread_ref[2 * m], spread_ref[2 * m + 1]) for m in range(3)]
@@ -343,6 +343,7 @@
     outer_ref,
     twist_ref,
     last_ref,
+    up_ref,
     down_ref,
     same_ref,
     crossed_ref,
@@ -615,6 +616,22 @@
         flops=10_000_000,
     )
     up = lax.ppermute(low, "gx", [(i, (i + 1) % DEV_X) for i in range(DEV_X)])
+    side, back_twist, back_last = call(
+        side_kernel,
+        (held(2, ROWS, SPAN), held(2, LANES, LANES), held(2, LANES, LANES)),
+        *groups,
+        SIDE_TABLE,
+        TABLES["back_twist"],
+        TABLES["back_last"],
+        spread,
+        loose=2,
+        waits=1,
+        scratch=[
+            pltpu.VMEM((SUBS + 2, 3, ROWS, LANES), jnp.float32),
+            pltpu.SemaphoreType.DMA((2,)),
+        ],
+        flops=30_000_000,
+    )
     back, high = call(
         column_kernel,
         (f32(3 * DEV_X, LANES), f32(3, TILE, SPAN)),
@@ -624,27 +641,11 @@
         col_twist,
         col_small,
         own,
-        up,
+        side,
         waits=1,
     )
     down = lax.ppermute(high, "gx", [((i + 1) % DEV_X, i) for i in range(DEV_X)])
     returned = all_to_all_x(back)
-    side, back_twist, back_last = call(
-        side_kernel,
-        (held(2, ROWS, SPAN), held(2, LANES, LANES), held(2, LANES, LANES)),
-        *groups,
-        SIDE_TABLE,
-        TABLES["back_twist"],
-        TABLES["back_last"],
-        back,
-        loose=2,
-        waits=1,
-        scratch=[
-            pltpu.VMEM((SUBS + 2, 3, ROWS, LANES), jnp.float32),
-            pltpu.SemaphoreType.DMA((2,)),
-        ],
-        flops=30_000_000,
-    )
     same, crossed = call(
         inverse_kernel,
         (f32(2, 2, ROWS, SPAN), f32(2, 2, ROWS, SPAN)),
@@ -653,8 +654,9 @@
         outer,
         back_twist,
         back_last,
+        up,
         down,
-        waits=1,
+        waits=2,
     )
     from_mate = lax.ppermute(crossed, "gy", mate_pairs)
     from_far = lax.ppermute(same[1] + from_mate[1], "gy", far_pairs)

time: 83.2 us -> 82.1 us (0.987)
  starting transfers between devices: 57.2 us -> 55.8 us
    all_to_all x2, waiting for transfers between devices: 1.44 us -> 9.75 us  [all_to_all_x(): lax.all_to_all(shaped, 'gx', split_axis=0, concat_axis=0, tiled=True)]
    ppermute x1, waiting for transfers between devices: 9.28 us -> 1.12 us  [local(): up = lax.ppermute(low, 'gx', [(i, (i + 1) % DEV_X) for i in range(DEV_X)])]
  transfers between devices with their start and end apart: 9 -> 9, of which waited for: 6 -> 5; matrix products, arithmetic and copies ran while one was open for 0% -> 0% of each run, Pallas kernels for 8% -> 8%
where the time goes in v2:
time: 82.1 us; the launch traced here: 81.6 us
  starting transfers between devices  55.8 us (68%)
  waiting for transfers between devices  13.2 us (16%)
  Pallas kernels  11.8 us (14%)
    all_to_all x2, starting transfers between devices, all_to_all_x(): lax.all_to_all(shaped, 'gx', split_axis=0, concat_axis=0, tiled=True)  21.3 us
    pallas_call x7, Pallas kernels, call(): pl.pallas_call(body, out_shape=shapes, in_specs=specs, out_specs=jax.tree...  11.8 us
    all_to_all x2, waiting for transfers between devices, all_to_all_x(): lax.all_to_all(shaped, 'gx', split_axis=0, concat_axis=0, tiled=True)  9.75 us
    ppermute x1, starting transfers between devices, local(): lax.ppermute(high, 'gx', [((i + 1) % DEV_X, i) for i in range(DEV_X)])  9.13 us
    ppermute x1, starting transfers between devices, local(): mate = lax.ppermute(own, 'gy', mate_pairs)  6.67 us
    ppermute x1, starting transfers between devices, local(): from_mate = lax.ppermute(crossed, 'gy', mate_pairs)  4.71 us
    ppermute x1, starting transfers between devices, local(): diagonal = lax.ppermute(far, 'gy', mate_pairs)  4.55 us
    ppermute x1, starting transfers between devices, local(): far = lax.ppermute(own, 'gy', far_pairs)  4.03 us
  transfers between devices with their start and end apart: 9, of which 5 were waited for; matrix products, arithmetic and copies ran while one was open for 0% of the time, Pallas kernels for 8%

profile of v2, /device:TPU:1, one launch (start us, length us, event | category | flops | bytes accessed | tf_op | source)
XLA Modules:
  0.0 81.6 jit_solution(9849612869823426780)
XLA Ops:
  0.0 0.0 copy-start
  0.0 1.2 %shard_map.136 = (f32[3,8,1024]{2,1,0:T(8,128)S(1)}, f32[2,128,128]{2,1,0:T(8,128)S(1)}, f32[2,64,128]{2,1,0:T(8,128)S(1)}, f32[2,128,256]{2,1,0:T(8,128)S(1)}) custom-call(f32[2,8,1024]{2,1,0:T(8,128)} %unknown_ref.1, f32[8,1024]{1,0:T(8,128)} %height_ref.1, f32[4,2,128,128]{3,2,1,0:T(8,128)} %constant.18.clone.first_ref, ...), custom_call_target="tpu_custom_call" | custom-call | flops 1000000 | bytes 1000000 | tf_op jit(solution)/shard_map/pallas_call | solution.py:247
  1.3 4.0 %collective-permute-start = (f32[3,8,1024]{2,1,0:T(8,128)S(1)}, f32[3,8,1024]{2,1,0:T(8,128)S(1)}, u32[]{:S(2)}, u32[]{:S(2)}) collective-permute-start(f32[3,8,1024]{2,1,0:T(8,128)S(1)} %get-tuple-element.21.own_ref), channel_id=1, source_target_pairs={{0,2},{1,3},{2,0},{3,1},{4,6},{5,7},{6,4},{7,5},{8,10},{9,11},{10,... | collective-permute-start | bytes 294920 | tf_op jit(solution)/shard_map/ppermute | solution.py:582
  5.3 6.7 %collective-permute-start.1 = (f32[3,8,1024]{2,1,0:T(8,128)S(1)}, f32[3,8,1024]{2,1,0:T(8,128)S(1)}, u32[]{:S(2)}, u32[]{:S(2)}) collective-permute-start(f32[3,8,1024]{2,1,0:T(8,128)S(1)} %get-tuple-element.21.own_ref), channel_id=1, source_target_pairs={{0,1},{1,0},{2,3},{3,2},{4,5},{5,4},{6,7},{7,6},{8,9},{9,8},{10,11... | collective-permute-start | bytes 294920 | tf_op jit(solution)/shard_map/ppermute | solution.py:583
  12.0 0.0 collective-permute-done.far_ref
  12.0 4.6 %collective-permute-start.2 = (f32[3,8,1024]{2,1,0:T(8,128)S(1)}, f32[3,8,1024]{2,1,0:T(8,128)S(1)}, u32[]{:S(2)}, u32[]{:S(2)}) collective-permute-start(f32[3,8,1024]{2,1,0:T(8,128)S(1)} %collective-permute-done.far_ref), channel_id=1, source_target_pairs={{0,1},{1,0},{2,3},{3,2},{4,5},{5,4},{6,7},{7,6},{8,9},{9,8},{10,11... | collective-permute-start | bytes 294920 | tf_op jit(solution)/shard_map/ppermute | solution.py:584
  16.5 0.0 collective-permute-done.1.mate_ref
  16.6 0.9 %collective-permute-done.2.diag_ref = f32[3,8,1024]{2,1,0:T(8,128)S(1)} collective-permute-done((f32[3,8,1024]{2,1,0:T(8,128)S(1)}, f32[3,8,1024]{2,1,0:T(8,128)S(1)}, u32[]{:S(2)}, u32[]{:S(2)}) %collective-permute-start.2) | collective-permute-done | bytes 98336 | tf_op jit(solution)/shard_map/ppermute | solution.py:584
  17.5 1.4 %shard_map.137 = (f32[384,128]{1,0:T(8,128)}, f32[3,4,1024]{2,1,0:T(4,128)S(1)}) custom-call(f32[3,8,1024]{2,1,0:T(8,128)S(1)} %get-tuple-element.21.own_ref, f32[3,8,1024]{2,1,0:T(8,128)S(1)} %collective-permute-done.far_ref, f32[3,8,1024]{2,1,0:T(8,128)S(1)} %collective-permute-done.1.mate_ref, f32[3,8,1024]{2,1,0:T(8,128)S(1)} %collective-permute-done.2.diag_ref, ...), custom_call_target="tpu_custom_call" | custom-call | flops 1000000 | bytes 1000000 | tf_op jit(solution)/shard_map/pallas_call | solution.py:247
  18.9 14.6 %all-to-all-start = ((f32[128,1,384]{2,1,0:T(1,128)}), f32[128,1,384]{2,1,0:T(1,128)S(1)}, u32[]{:S(2)}, u32[]{:S(2)}) async-start(f32[128,1,384]{2,1,0:T(1,128)} %bitcast), calls=%async_computation | async-start | bytes 393216 | tf_op jit(solution)/shard_map/all_to_all | solution.py:559
  33.5 1.3 %shard_map.138 = (f32[6,128,128]{2,1,0:T(8,128)S(1)}, f32[2,128,128]{2,1,0:T(8,128)S(1)}, f32[2,2,128,128]{3,2,1,0:T(8,128)S(1)}) custom-call(f32[128,128]{1,0:T(8,128)} %bitcast.23, f32[128,128]{1,0:T(8,128)} %bitcast.24, f32[128,128]{1,0:T(8,128)} %bitcast.25, f32[2,128,128]{2,1,0:T(8,128)} %constant.21.clone.twist_ref, ...), custom_call_target="tpu_custom_call" | custom-call | flops 10000000 | bytes 1000000 | tf_op jit(solution)/shard_map/pallas_call | solution.py:247
  34.8 0.0 copy-done
  34.8 3.1 %shard_map.139 = (f32[2,8,1024]{2,1,0:T(8,128)S(1)}, f32[2,128,128]{2,1,0:T(8,128)S(1)}, f32[2,128,128]{2,1,0:T(8,128)S(1)}) custom-call(f32[3,8,1024]{2,1,0:T(8,128)S(1)} %get-tuple-element.21.own_ref, f32[3,8,1024]{2,1,0:T(8,128)S(1)} %collective-permute-done.far_ref, f32[3,8,1024]{2,1,0:T(8,128)S(1)} %collective-permute-done.1.mate_ref, ...), custom_call_target="tpu_custom_call" | custom-call | flops 30000000 | bytes 1000000 | tf_op jit(solution)/shard_map/pallas_call | solution.py:247
  37.9 9.8 %all-to-all-done = f32[128,1,384]{2,1,0:T(1,128)S(1)} async-done(((f32[128,1,384]{2,1,0:T(1,128)}), f32[128,1,384]{2,1,0:T(1,128)S(1)}, u32[]{:S(2)}, u32[]{:S(2)}) %all-to-all-start) | async-done | bytes 196640 | tf_op jit(solution)/shard_map/all_to_all | solution.py:559
  47.7 0.0 copy-start.1
  47.7 2.0 %shard_map.140 = (f32[384,128]{1,0:T(8,128)}, f32[3,4,1024]{2,1,0:T(4,128)S(1)}) custom-call(f32[384,128]{1,0:T(8,128)S(1)} %bitcast.22, f32[6,128,128]{2,1,0:T(8,128)S(1)} %get-tuple-element.27.after_ref.spread_ref, f32[2,128,256]{2,1,0:T(8,128)S(1)} %get-tuple-element.24.outer_ref, f32[2,128,128]{2,1,0:T(8,128)S(1)} %get-tuple-element.28.twist_ref, ...), custom_call_target="tpu_custom_call" | custom-call | flops 1000000 | bytes 1000000 | tf_op jit(solution)/shard_map/pallas_call | solution.py:247
  49.7 6.7 %all-to-all-start.1 = ((f32[128,1,384]{2,1,0:T(1,128)}), f32[128,1,384]{2,1,0:T(1,128)S(1)}, u32[]{:S(2)}, u32[]{:S(2)}) async-start(f32[128,1,384]{2,1,0:T(1,128)} %bitcast.11), calls=%async_computation.1 | async-start | bytes 393216 | tf_op jit(solution)/shard_map/all_to_all | solution.py:559
  56.4 2.5 %collective-permute-start.3 = (f32[3,4,1024]{2,1,0:T(4,128)S(1)}, f32[3,4,1024]{2,1,0:T(4,128)S(1)}, u32[]{:S(2)}, u32[]{:S(2)}) collective-permute-start(f32[3,4,1024]{2,1,0:T(4,128)S(1)} %get-tuple-element.25), channel_id=1, source_target_pairs={{0,4},{4,8},{8,12},{12,16},{16,20},{20,24},{24,28},{28,32},{32,36}... | collective-permute-start | bytes 147464 | tf_op jit(solution)/shard_map/ppermute | solution.py:618
  58.9 9.1 %collective-permute-start.4 = (f32[3,4,1024]{2,1,0:T(4,128)S(1)}, f32[3,4,1024]{2,1,0:T(4,128)S(1)}, u32[]{:S(2)}, u32[]{:S(2)}) collective-permute-start(f32[3,4,1024]{2,1,0:T(4,128)S(1)} %get-tuple-element.31), channel_id=1, source_target_pairs={{4,0},{8,4},{12,8},{16,12},{20,16},{24,20},{28,24},{32,28},{36,32}... | collective-permute-start | bytes 147464 | tf_op jit(solution)/shard_map/ppermute | solution.py:647
  68.1 1.1 %collective-permute-done.3.up_ref = f32[3,4,1024]{2,1,0:T(4,128)S(1)} collective-permute-done((f32[3,4,1024]{2,1,0:T(4,128)S(1)}, f32[3,4,1024]{2,1,0:T(4,128)S(1)}, u32[]{:S(2)}, u32[]{:S(2)}) %collective-permute-start.3) | collective-permute-done | bytes 49184 | tf_op jit(solution)/shard_map/ppermute | solution.py:618
  69.2 0.4 collective-permute-done.4.down_ref
  69.6 0.0 all-to-all-done.1
  69.6 0.7 shard_map.141
  70.3 4.7 %collective-permute-start.5 = (f32[2,2,8,1024]{3,2,1,0:T(8,128)S(1)}, f32[2,2,8,1024]{3,2,1,0:T(8,128)S(1)}, u32[]{:S(2)}, u32[]{:S(2)}) collective-permute-start(f32[2,2,8,1024]{3,2,1,0:T(8,128)S(1)} %get-tuple-element.36), channel_id=1, source_target_pairs={{0,1},{1,0},{2,3},{3,2},{4,5},{5,4},{6,7},{7,6},{8,9},{9,8},{10,11... | collective-permute-start | bytes 393224 | tf_op jit(solution)/shard_map/ppermute | solution.py:661
  75.0 1.0 %collective-permute-done.5.mate_ref = f32[2,2,8,1024]{3,2,1,0:T(8,128)S(1)} collective-permute-done((f32[2,2,8,1024]{3,2,1,0:T(8,128)S(1)}, f32[2,2,8,1024]{3,2,1,0:T(8,128)S(1)}, u32[]{:S(2)}, u32[]{:S(2)}) %collective-permute-start.5) | collective-permute-done | bytes 131104 | tf_op jit(solution)/shard_map/ppermute | solution.py:661
  76.0 2.9 %collective-permute-start.6 = (f32[2,8,1024]{2,1,0:T(8,128)S(1)}, f32[2,8,1024]{2,1,0:T(8,128)S(1)}, u32[]{:S(2)}, u32[]{:S(2)}) collective-permute-start(f32[2,8,1024]{2,1,0:T(8,128)S(1)} %fusion), channel_id=1, source_target_pairs={{0,2},{1,3},{2,0},{3,1},{4,6},{5,7},{6,4},{7,5},{8,10},{9,11},{10,... | collective-permute-start | bytes 196616 | tf_op jit(solution)/shard_map/ppermute | solution.py:662
  78.9 0.0 copy-done.1
  78.9 2.0 %shard_map.142 = f32[2,8,1024]{2,1,0:T(8,128)S(1)} custom-call(f32[3,8,1024]{2,1,0:T(8,128)S(1)} %get-tuple-element.21.own_ref, f32[3,4,1024]{2,1,0:T(4,128)S(1)} %collective-permute-done.3.up_ref, f32[3,4,1024]{2,1,0:T(4,128)S(1)} %collective-permute-done.4.down_ref, f32[32,7,8,128]{3,2,1,0:T(8,128)S(1)} %copy-done.1, ...), custom_call_target="tpu_custom_call" | custom-call | flops 20000000 | bytes 1000000 | tf_op jit(solution)/shard_map/pallas_call | solution.py:247
  81.0 0.0 collective-permute-done.6
  81.0 0.6 add.11
  (1 shorter events, 0.0 us)
Async XLA Ops:
  0.0 34.8 %copy-start = (f32[48,7,8,128]{3,2,1,0:T(8,128)S(1)}, f32[48,7,8,128]{3,2,1,0:T(8,128)}, u32[]{:S(2)}) copy-start(f32[48,7,8,128]{3,2,1,0:T(8,128)} %constant.25.clone.table_ref) | copy-start | bytes 4128772
  1.3 10.7 %collective-permute-start = (f32[3,8,1024]{2,1,0:T(8,128)S(1)}, f32[3,8,1024]{2,1,0:T(8,128)S(1)}, u32[]{:S(2)}, u32[]{:S(2)}) collective-permute-start(f32[3,8,1024]{2,1,0:T(8,128)S(1)} %get-tuple-element.21.own_ref), channel_id=1, source_target_pairs={{0,2},{1,3},{2,0},{3,1},{4,6},{5,7},{6,4},{7,5},{8,10},{9,11},{10,... | collective-permute-start | bytes 294920 | tf_op jit(solution)/shard_map/ppermute | solution.py:582
  5.3 11.3 %collective-permute-start.1 = (f32[3,8,1024]{2,1,0:T(8,128)S(1)}, f32[3,8,1024]{2,1,0:T(8,128)S(1)}, u32[]{:S(2)}, u32[]{:S(2)}) collective-permute-start(f32[3,8,1024]{2,1,0:T(8,128)S(1)} %get-tuple-element.21.own_ref), channel_id=1, source_target_pairs={{0,1},{1,0},{2,3},{3,2},{4,5},{5,4},{6,7},{7,6},{8,9},{9,8},{10,11... | collective-permute-start | bytes 294920 | tf_op jit(solution)/shard_map/ppermute | solution.py:583
  12.0 5.5 %collective-permute-start.2 = (f32[3,8,1024]{2,1,0:T(8,128)S(1)}, f32[3,8,1024]{2,1,0:T(8,128)S(1)}, u32[]{:S(2)}, u32[]{:S(2)}) collective-permute-start(f32[3,8,1024]{2,1,0:T(8,128)S(1)} %collective-permute-done.far_ref), channel_id=1, source_target_pairs={{0,1},{1,0},{2,3},{3,2},{4,5},{5,4},{6,7},{7,6},{8,9},{9,8},{10,11... | collective-permute-start | bytes 294920 | tf_op jit(solution)/shard_map/ppermute | solution.py:584
  18.9 28.8 %all-to-all-start = ((f32[128,1,384]{2,1,0:T(1,128)}), f32[128,1,384]{2,1,0:T(1,128)S(1)}, u32[]{:S(2)}, u32[]{:S(2)}) async-start(f32[128,1,384]{2,1,0:T(1,128)} %bitcast), calls=%async_computation | async-start | bytes 393216 | tf_op jit(solution)/shard_map/all_to_all | solution.py:559
  47.7 31.2 %copy-start.1 = (f32[32,7,8,128]{3,2,1,0:T(8,128)S(1)}, f32[32,7,8,128]{3,2,1,0:T(8,128)}, u32[]{:S(2)}) copy-start(f32[32,7,8,128]{3,2,1,0:T(8,128)} %constant.26.clone.table_ref) | copy-start | bytes 2752516
  49.7 19.9 %all-to-all-start.1 = ((f32[128,1,384]{2,1,0:T(1,128)}), f32[128,1,384]{2,1,0:T(1,128)S(1)}, u32[]{:S(2)}, u32[]{:S(2)}) async-start(f32[128,1,384]{2,1,0:T(1,128)} %bitcast.11), calls=%async_computation.1 | async-start | bytes 393216 | tf_op jit(solution)/shard_map/all_to_all | solution.py:559
  56.4 12.7 %collective-permute-start.3 = (f32[3,4,1024]{2,1,0:T(4,128)S(1)}, f32[3,4,1024]{2,1,0:T(4,128)S(1)}, u32[]{:S(2)}, u32[]{:S(2)}) collective-permute-start(f32[3,4,1024]{2,1,0:T(4,128)S(1)} %get-tuple-element.25), channel_id=1, source_target_pairs={{0,4},{4,8},{8,12},{12,16},{16,20},{20,24},{24,28},{28,32},{32,36}... | collective-permute-start | bytes 147464 | tf_op jit(solution)/shard_map/ppermute | solution.py:618
  58.9 10.7 %collective-permute-start.4 = (f32[3,4,1024]{2,1,0:T(4,128)S(1)}, f32[3,4,1024]{2,1,0:T(4,128)S(1)}, u32[]{:S(2)}, u32[]{:S(2)}) collective-permute-start(f32[3,4,1024]{2,1,0:T(4,128)S(1)} %get-tuple-element.31), channel_id=1, source_target_pairs={{4,0},{8,4},{12,8},{16,12},{20,16},{24,20},{28,24},{32,28},{36,32}... | collective-permute-start | bytes 147464 | tf_op jit(solution)/shard_map/ppermute | solution.py:647
  70.3 5.7 %collective-permute-start.5 = (f32[2,2,8,1024]{3,2,1,0:T(8,128)S(1)}, f32[2,2,8,1024]{3,2,1,0:T(8,128)S(1)}, u32[]{:S(2)}, u32[]{:S(2)}) collective-permute-start(f32[2,2,8,1024]{3,2,1,0:T(8,128)S(1)} %get-tuple-element.36), channel_id=1, source_target_pairs={{0,1},{1,0},{2,3},{3,2},{4,5},{5,4},{6,7},{7,6},{8,9},{9,8},{10,11... | collective-permute-start | bytes 393224 | tf_op jit(solution)/shard_map/ppermute | solution.py:661
  76.0 5.0 %collective-permute-start.6 = (f32[2,8,1024]{2,1,0:T(8,128)S(1)}, f32[2,8,1024]{2,1,0:T(8,128)S(1)}, u32[]{:S(2)}, u32[]{:S(2)}) collective-permute-start(f32[2,8,1024]{2,1,0:T(8,128)S(1)} %fusion), channel_id=1, source_target_pairs={{0,2},{1,3},{2,0},{3,1},{4,6},{5,7},{6,4},{7,5},{8,10},{9,11},{10,... | collective-permute-start | bytes 196616 | tf_op jit(solution)/shard_map/ppermute | solution.py:662

commit v3 on v2

--- a/solution.py
+++ b/solution.py
@@ -98,7 +98,9 @@
     def one(x, y):
         return lax.dot_general(x, y, (dims, ((), ())), preferred_element_type=jnp.float32)
 
-    return one(left[0], right[0]) + (one(left[0], right[1]) + one(left[1], right[0]))
+    rows = left[0].shape[0]
+    both = one(jnp.concatenate(left, 0), right[0])
+    return both[:rows] + (one(left[0], right[1]) + both[rows:])
 
 
 def dot(left, right):

time: 82.1 us -> 82 us (level)
  no operation moved by 1% of the time
where the time goes in v3:
time: 82 us; the launch traced here: 81.5 us
  starting transfers between devices  55.8 us (68%)
  waiting for transfers between devices  13.3 us (16%)
  Pallas kernels  11.7 us (14%)
    all_to_all x2, starting transfers between devices, all_to_all_x(): lax.all_to_all(shaped, 'gx', split_axis=0, concat_axis=0, tiled=True)  21.3 us
    pallas_call x7, Pallas kernels, call(): pl.pallas_call(body, out_shape=shapes, in_specs=specs, out_specs=jax.tree...  11.7 us
    all_to_all x2, waiting for transfers between devices, all_to_all_x(): lax.all_to_all(shaped, 'gx', split_axis=0, concat_axis=0, tiled=True)  9.81 us
    ppermute x1, starting transfers between devices, local(): lax.ppermute(high, 'gx', [((i + 1) % DEV_X, i) for i in range(DEV_X)])  9.13 us
    ppermute x1, starting transfers between devices, local(): mate = lax.ppermute(own, 'gy', mate_pairs)  6.67 us
    ppermute x1, starting transfers between devices, local(): from_mate = lax.ppermute(crossed, 'gy', mate_pairs)  4.72 us
    ppermute x1, starting transfers between devices, local(): diagonal = lax.ppermute(far, 'gy', mate_pairs)  4.55 us
    ppermute x1, starting transfers between devices, local(): far = lax.ppermute(own, 'gy', far_pairs)  4.03 us
  transfers between devices with their start and end apart: 9, of which 5 were waited for; matrix products, arithmetic and copies ran while one was open for 0% of the time, Pallas kernels for 8%

profile of v3, /device:TPU:1, one launch (start us, length us, event | category | flops | bytes accessed | tf_op | source)
XLA Modules:
  0.0 81.5 jit_solution(9764574282537639708)
XLA Ops:
  0.0 0.0 copy-start
  0.0 1.2 %shard_map.136 = (f32[3,8,1024]{2,1,0:T(8,128)S(1)}, f32[2,128,128]{2,1,0:T(8,128)S(1)}, f32[2,64,128]{2,1,0:T(8,128)S(1)}, f32[2,128,256]{2,1,0:T(8,128)S(1)}) custom-call(f32[2,8,1024]{2,1,0:T(8,128)} %unknown_ref.1, f32[8,1024]{1,0:T(8,128)} %height_ref.1, f32[4,2,128,128]{3,2,1,0:T(8,128)} %constant.18.clone.first_ref, ...), custom_call_target="tpu_custom_call" | custom-call | flops 1000000 | bytes 1000000 | tf_op jit(solution)/shard_map/pallas_call | solution.py:249
  1.3 4.0 %collective-permute-start = (f32[3,8,1024]{2,1,0:T(8,128)S(1)}, f32[3,8,1024]{2,1,0:T(8,128)S(1)}, u32[]{:S(2)}, u32[]{:S(2)}) collective-permute-start(f32[3,8,1024]{2,1,0:T(8,128)S(1)} %get-tuple-element.21.own_ref), channel_id=1, source_target_pairs={{0,2},{1,3},{2,0},{3,1},{4,6},{5,7},{6,4},{7,5},{8,10},{9,11},{10,... | collective-permute-start | bytes 294920 | tf_op jit(solution)/shard_map/ppermute | solution.py:584
  5.3 6.7 %collective-permute-start.1 = (f32[3,8,1024]{2,1,0:T(8,128)S(1)}, f32[3,8,1024]{2,1,0:T(8,128)S(1)}, u32[]{:S(2)}, u32[]{:S(2)}) collective-permute-start(f32[3,8,1024]{2,1,0:T(8,128)S(1)} %get-tuple-element.21.own_ref), channel_id=1, source_target_pairs={{0,1},{1,0},{2,3},{3,2},{4,5},{5,4},{6,7},{7,6},{8,9},{9,8},{10,11... | collective-permute-start | bytes 294920 | tf_op jit(solution)/shard_map/ppermute | solution.py:585
  12.0 0.0 collective-permute-done.far_ref
  12.0 4.6 %collective-permute-start.2 = (f32[3,8,1024]{2,1,0:T(8,128)S(1)}, f32[3,8,1024]{2,1,0:T(8,128)S(1)}, u32[]{:S(2)}, u32[]{:S(2)}) collective-permute-start(f32[3,8,1024]{2,1,0:T(8,128)S(1)} %collective-permute-done.far_ref), channel_id=1, source_target_pairs={{0,1},{1,0},{2,3},{3,2},{4,5},{5,4},{6,7},{7,6},{8,9},{9,8},{10,11... | collective-permute-start | bytes 294920 | tf_op jit(solution)/shard_map/ppermute | solution.py:586
  16.5 0.0 collective-permute-done.1.mate_ref
  16.6 0.9 %collective-permute-done.2.diag_ref = f32[3,8,1024]{2,1,0:T(8,128)S(1)} collective-permute-done((f32[3,8,1024]{2,1,0:T(8,128)S(1)}, f32[3,8,1024]{2,1,0:T(8,128)S(1)}, u32[]{:S(2)}, u32[]{:S(2)}) %collective-permute-start.2) | collective-permute-done | bytes 98336 | tf_op jit(solution)/shard_map/ppermute | solution.py:586
  17.5 1.3 %shard_map.137 = (f32[384,128]{1,0:T(8,128)}, f32[3,4,1024]{2,1,0:T(4,128)S(1)}) custom-call(f32[3,8,1024]{2,1,0:T(8,128)S(1)} %get-tuple-element.21.own_ref, f32[3,8,1024]{2,1,0:T(8,128)S(1)} %collective-permute-done.far_ref, f32[3,8,1024]{2,1,0:T(8,128)S(1)} %collective-permute-done.1.mate_ref, f32[3,8,1024]{2,1,0:T(8,128)S(1)} %collective-permute-done.2.diag_ref, ...), custom_call_target="tpu_custom_call" | custom-call | flops 1000000 | bytes 1000000 | tf_op jit(solution)/shard_map/pallas_call | solution.py:249
  18.8 14.6 %all-to-all-start = ((f32[128,1,384]{2,1,0:T(1,128)}), f32[128,1,384]{2,1,0:T(1,128)S(1)}, u32[]{:S(2)}, u32[]{:S(2)}) async-start(f32[128,1,384]{2,1,0:T(1,128)} %bitcast), calls=%async_computation | async-start | bytes 393216 | tf_op jit(solution)/shard_map/all_to_all | solution.py:561
  33.4 1.3 %shard_map.138 = (f32[6,128,128]{2,1,0:T(8,128)S(1)}, f32[2,128,128]{2,1,0:T(8,128)S(1)}, f32[2,2,128,128]{3,2,1,0:T(8,128)S(1)}) custom-call(f32[128,128]{1,0:T(8,128)} %bitcast.23, f32[128,128]{1,0:T(8,128)} %bitcast.24, f32[128,128]{1,0:T(8,128)} %bitcast.25, f32[2,128,128]{2,1,0:T(8,128)} %constant.21.clone.twist_ref, ...), custom_call_target="tpu_custom_call" | custom-call | flops 10000000 | bytes 1000000 | tf_op jit(solution)/shard_map/pallas_call | solution.py:249
  34.7 0.0 copy-done
  34.7 3.1 %shard_map.139 = (f32[2,8,1024]{2,1,0:T(8,128)S(1)}, f32[2,128,128]{2,1,0:T(8,128)S(1)}, f32[2,128,128]{2,1,0:T(8,128)S(1)}) custom-call(f32[3,8,1024]{2,1,0:T(8,128)S(1)} %get-tuple-element.21.own_ref, f32[3,8,1024]{2,1,0:T(8,128)S(1)} %collective-permute-done.far_ref, f32[3,8,1024]{2,1,0:T(8,128)S(1)} %collective-permute-done.1.mate_ref, ...), custom_call_target="tpu_custom_call" | custom-call | flops 30000000 | bytes 1000000 | tf_op jit(solution)/shard_map/pallas_call | solution.py:249
  37.8 9.8 %all-to-all-done = f32[128,1,384]{2,1,0:T(1,128)S(1)} async-done(((f32[128,1,384]{2,1,0:T(1,128)}), f32[128,1,384]{2,1,0:T(1,128)S(1)}, u32[]{:S(2)}, u32[]{:S(2)}) %all-to-all-start) | async-done | bytes 196640 | tf_op jit(solution)/shard_map/all_to_all | solution.py:561
  47.6 0.0 copy-start.1
  47.6 2.0 %shard_map.140 = (f32[384,128]{1,0:T(8,128)}, f32[3,4,1024]{2,1,0:T(4,128)S(1)}) custom-call(f32[384,128]{1,0:T(8,128)S(1)} %bitcast.22, f32[6,128,128]{2,1,0:T(8,128)S(1)} %get-tuple-element.27.after_ref.spread_ref, f32[2,128,256]{2,1,0:T(8,128)S(1)} %get-tuple-element.24.outer_ref, f32[2,128,128]{2,1,0:T(8,128)S(1)} %get-tuple-element.28.twist_ref, ...), custom_call_target="tpu_custom_call" | custom-call | flops 1000000 | bytes 1000000 | tf_op jit(solution)/shard_map/pallas_call | solution.py:249
  49.7 6.7 %all-to-all-start.1 = ((f32[128,1,384]{2,1,0:T(1,128)}), f32[128,1,384]{2,1,0:T(1,128)S(1)}, u32[]{:S(2)}, u32[]{:S(2)}) async-start(f32[128,1,384]{2,1,0:T(1,128)} %bitcast.11), calls=%async_computation.1 | async-start | bytes 393216 | tf_op jit(solution)/shard_map/all_to_all | solution.py:561
  56.3 2.5 %collective-permute-start.3 = (f32[3,4,1024]{2,1,0:T(4,128)S(1)}, f32[3,4,1024]{2,1,0:T(4,128)S(1)}, u32[]{:S(2)}, u32[]{:S(2)}) collective-permute-start(f32[3,4,1024]{2,1,0:T(4,128)S(1)} %get-tuple-element.25), channel_id=1, source_target_pairs={{0,4},{4,8},{8,12},{12,16},{16,20},{20,24},{24,28},{28,32},{32,36}... | collective-permute-start | bytes 147464 | tf_op jit(solution)/shard_map/ppermute | solution.py:620
  58.8 9.1 %collective-permute-start.4 = (f32[3,4,1024]{2,1,0:T(4,128)S(1)}, f32[3,4,1024]{2,1,0:T(4,128)S(1)}, u32[]{:S(2)}, u32[]{:S(2)}) collective-permute-start(f32[3,4,1024]{2,1,0:T(4,128)S(1)} %get-tuple-element.31), channel_id=1, source_target_pairs={{4,0},{8,4},{12,8},{16,12},{20,16},{24,20},{28,24},{32,28},{36,32}... | collective-permute-start | bytes 147464 | tf_op jit(solution)/shard_map/ppermute | solution.py:649
  68.0 1.0 %collective-permute-done.3.up_ref = f32[3,4,1024]{2,1,0:T(4,128)S(1)} collective-permute-done((f32[3,4,1024]{2,1,0:T(4,128)S(1)}, f32[3,4,1024]{2,1,0:T(4,128)S(1)}, u32[]{:S(2)}, u32[]{:S(2)}) %collective-permute-start.3) | collective-permute-done | bytes 49184 | tf_op jit(solution)/shard_map/ppermute | solution.py:620
  69.0 0.5 collective-permute-done.4.down_ref
  69.5 0.0 all-to-all-done.1
  69.5 0.7 shard_map.141
  70.2 4.7 %collective-permute-start.5 = (f32[2,2,8,1024]{3,2,1,0:T(8,128)S(1)}, f32[2,2,8,1024]{3,2,1,0:T(8,128)S(1)}, u32[]{:S(2)}, u32[]{:S(2)}) collective-permute-start(f32[2,2,8,1024]{3,2,1,0:T(8,128)S(1)} %get-tuple-element.36), channel_id=1, source_target_pairs={{0,1},{1,0},{2,3},{3,2},{4,5},{5,4},{6,7},{7,6},{8,9},{9,8},{10,11... | collective-permute-start | bytes 393224 | tf_op jit(solution)/shard_map/ppermute | solution.py:663
  74.9 1.0 %collective-permute-done.5.mate_ref = f32[2,2,8,1024]{3,2,1,0:T(8,128)S(1)} collective-permute-done((f32[2,2,8,1024]{3,2,1,0:T(8,128)S(1)}, f32[2,2,8,1024]{3,2,1,0:T(8,128)S(1)}, u32[]{:S(2)}, u32[]{:S(2)}) %collective-permute-start.5) | collective-permute-done | bytes 131104 | tf_op jit(solution)/shard_map/ppermute | solution.py:663
  75.9 2.9 %collective-permute-start.6 = (f32[2,8,1024]{2,1,0:T(8,128)S(1)}, f32[2,8,1024]{2,1,0:T(8,128)S(1)}, u32[]{:S(2)}, u32[]{:S(2)}) collective-permute-start(f32[2,8,1024]{2,1,0:T(8,128)S(1)} %fusion), channel_id=1, source_target_pairs={{0,2},{1,3},{2,0},{3,1},{4,6},{5,7},{6,4},{7,5},{8,10},{9,11},{10,... | collective-permute-start | bytes 196616 | tf_op jit(solution)/shard_map/ppermute | solution.py:664
  78.8 0.0 copy-done.1
  78.8 2.0 %shard_map.142 = f32[2,8,1024]{2,1,0:T(8,128)S(1)} custom-call(f32[3,8,1024]{2,1,0:T(8,128)S(1)} %get-tuple-element.21.own_ref, f32[3,4,1024]{2,1,0:T(4,128)S(1)} %collective-permute-done.3.up_ref, f32[3,4,1024]{2,1,0:T(4,128)S(1)} %collective-permute-done.4.down_ref, f32[32,7,8,128]{3,2,1,0:T(8,128)S(1)} %copy-done.1, ...), custom_call_target="tpu_custom_call" | custom-call | flops 20000000 | bytes 1000000 | tf_op jit(solution)/shard_map/pallas_call | solution.py:249
  80.8 0.0 collective-permute-done.6
  80.9 0.6 add.11
  (1 shorter events, 0.0 us)
Async XLA Ops:
  0.0 34.7 %copy-start = (f32[48,7,8,128]{3,2,1,0:T(8,128)S(1)}, f32[48,7,8,128]{3,2,1,0:T(8,128)}, u32[]{:S(2)}) copy-start(f32[48,7,8,128]{3,2,1,0:T(8,128)} %constant.25.clone.table_ref) | copy-start | bytes 4128772
  1.3 10.7 %collective-permute-start = (f32[3,8,1024]{2,1,0:T(8,128)S(1)}, f32[3,8,1024]{2,1,0:T(8,128)S(1)}, u32[]{:S(2)}, u32[]{:S(2)}) collective-permute-start(f32[3,8,1024]{2,1,0:T(8,128)S(1)} %get-tuple-element.21.own_ref), channel_id=1, source_target_pairs={{0,2},{1,3},{2,0},{3,1},{4,6},{5,7},{6,4},{7,5},{8,10},{9,11},{10,... | collective-permute-start | bytes 294920 | tf_op jit(solution)/shard_map/ppermute | solution.py:584
  5.3 11.3 %collective-permute-start.1 = (f32[3,8,1024]{2,1,0:T(8,128)S(1)}, f32[3,8,1024]{2,1,0:T(8,128)S(1)}, u32[]{:S(2)}, u32[]{:S(2)}) collective-permute-start(f32[3,8,1024]{2,1,0:T(8,128)S(1)} %get-tuple-element.21.own_ref), channel_id=1, source_target_pairs={{0,1},{1,0},{2,3},{3,2},{4,5},{5,4},{6,7},{7,6},{8,9},{9,8},{10,11... | collective-permute-start | bytes 294920 | tf_op jit(solution)/shard_map/ppermute | solution.py:585
  12.0 5.5 %collective-permute-start.2 = (f32[3,8,1024]{2,1,0:T(8,128)S(1)}, f32[3,8,1024]{2,1,0:T(8,128)S(1)}, u32[]{:S(2)}, u32[]{:S(2)}) collective-permute-start(f32[3,8,1024]{2,1,0:T(8,128)S(1)} %collective-permute-done.far_ref), channel_id=1, source_target_pairs={{0,1},{1,0},{2,3},{3,2},{4,5},{5,4},{6,7},{7,6},{8,9},{9,8},{10,11... | collective-permute-start | bytes 294920 | tf_op jit(solution)/shard_map/ppermute | solution.py:586
  18.8 28.9 %all-to-all-start = ((f32[128,1,384]{2,1,0:T(1,128)}), f32[128,1,384]{2,1,0:T(1,128)S(1)}, u32[]{:S(2)}, u32[]{:S(2)}) async-start(f32[128,1,384]{2,1,0:T(1,128)} %bitcast), calls=%async_computation | async-start | bytes 393216 | tf_op jit(solution)/shard_map/all_to_all | solution.py:561
  47.6 31.1 %copy-start.1 = (f32[32,7,8,128]{3,2,1,0:T(8,128)S(1)}, f32[32,7,8,128]{3,2,1,0:T(8,128)}, u32[]{:S(2)}) copy-start(f32[32,7,8,128]{3,2,1,0:T(8,128)} %constant.26.clone.table_ref) | copy-start | bytes 2752516
  49.7 19.8 %all-to-all-start.1 = ((f32[128,1,384]{2,1,0:T(1,128)}), f32[128,1,384]{2,1,0:T(1,128)S(1)}, u32[]{:S(2)}, u32[]{:S(2)}) async-start(f32[128,1,384]{2,1,0:T(1,128)} %bitcast.11), calls=%async_computation.1 | async-start | bytes 393216 | tf_op jit(solution)/shard_map/all_to_all | solution.py:561
  56.3 12.7 %collective-permute-start.3 = (f32[3,4,1024]{2,1,0:T(4,128)S(1)}, f32[3,4,1024]{2,1,0:T(4,128)S(1)}, u32[]{:S(2)}, u32[]{:S(2)}) collective-permute-start(f32[3,4,1024]{2,1,0:T(4,128)S(1)} %get-tuple-element.25), channel_id=1, source_target_pairs={{0,4},{4,8},{8,12},{12,16},{16,20},{20,24},{24,28},{28,32},{32,36}... | collective-permute-start | bytes 147464 | tf_op jit(solution)/shard_map/ppermute | solution.py:620
  58.8 10.7 %collective-permute-start.4 = (f32[3,4,1024]{2,1,0:T(4,128)S(1)}, f32[3,4,1024]{2,1,0:T(4,128)S(1)}, u32[]{:S(2)}, u32[]{:S(2)}) collective-permute-start(f32[3,4,1024]{2,1,0:T(4,128)S(1)} %get-tuple-element.31), channel_id=1, source_target_pairs={{4,0},{8,4},{12,8},{16,12},{20,16},{24,20},{28,24},{32,28},{36,32}... | collective-permute-start | bytes 147464 | tf_op jit(solution)/shard_map/ppermute | solution.py:649
  70.2 5.7 %collective-permute-start.5 = (f32[2,2,8,1024]{3,2,1,0:T(8,128)S(1)}, f32[2,2,8,1024]{3,2,1,0:T(8,128)S(1)}, u32[]{:S(2)}, u32[]{:S(2)}) collective-permute-start(f32[2,2,8,1024]{3,2,1,0:T(8,128)S(1)} %get-tuple-element.36), channel_id=1, source_target_pairs={{0,1},{1,0},{2,3},{3,2},{4,5},{5,4},{6,7},{7,6},{8,9},{9,8},{10,11... | collective-permute-start | bytes 393224 | tf_op jit(solution)/shard_map/ppermute | solution.py:663
  75.9 5.0 %collective-permute-start.6 = (f32[2,8,1024]{2,1,0:T(8,128)S(1)}, f32[2,8,1024]{2,1,0:T(8,128)S(1)}, u32[]{:S(2)}, u32[]{:S(2)}) collective-permute-start(f32[2,8,1024]{2,1,0:T(8,128)S(1)} %fusion), channel_id=1, source_target_pairs={{0,2},{1,3},{2,0},{3,1},{4,6},{5,7},{6,4},{7,5},{8,10},{9,11},{10,... | collective-permute-start | bytes 196616 | tf_op jit(solution)/shard_map/ppermute | solution.py:664
